TPU v7x, 32 devices: a whole 2x2x4 slice. The times are simulated.
32 devices in a mesh: replica: 4 (over y, x), shard: 8 (over z, core).
Axes of the slice: x: 2, y: 2, z: 4, core: 2. Of those that a mesh axis runs over, the one named last changes fastest.
Arguments:
- tokens: bfloat16 [24576, 960], P(('replica', 'shard')), may hold values from -6 to 6
- cotangent: bfloat16 [24576, 960], P(('replica', 'shard')), may hold values from -6 to 6
- seq_lengths: int32 [32, 4], P(('replica', 'shard')), may hold values from 0 to 512, as said below
- w_query: bfloat16 [960, 960], P('shard'), may hold values from -0.1875 to 0.1875
- key_weight: bfloat16 [960, 320], P('shard'), may hold values from -0.1875 to 0.1875
- value_weight: bfloat16 [960, 320], P('shard'), may hold values from -0.1875 to 0.1875
- w_out: bfloat16 [960, 960], P('shard'), may hold values from -0.75 to 0.75
- w_gate: bfloat16 [960, 2560], P('shard'), may hold values from -0.1875 to 0.1875
- w_up: bfloat16 [960, 2560], P('shard'), may hold values from -0.1875 to 0.1875
- w_down: bfloat16 [2560, 960], P('shard'), may hold values from -0.125 to 0.125
- gain_attn: bfloat16 [960], P('shard'), may hold values from 0.5 to 1.5
- gain_ffn: bfloat16 [960], P('shard'), may hold values from 0.5 to 1.5
Outputs:
- output: bfloat16 [24576, 960], P(('replica', 'shard'))
- grad_tokens: bfloat16 [24576, 960], P(('replica', 'shard'))
- grad_query: float32 [960, 960], P('shard')
- grad_key: float32 [960, 320], P('shard')
- grad_value: float32 [960, 320], P('shard')
- grad_out: float32 [960, 960], P('shard')
- grad_gate: float32 [960, 2560], P('shard')
- grad_up: float32 [960, 2560], P('shard')
- grad_down: float32 [2560, 960], P('shard')
- grad_gain_attn: float32 [960], P('shard')
- grad_gain_ffn: float32 [960], P('shard')
Inputs may be any that keep to these rules, and one draw needn't show every extreme that they name: `seq_lengths`: the lengths of one buffer sum to at most 768; unused slots hold 0; some buffer holds one sequence of exactly 512.
All inputs are finite; a program needn't handle non-finite values.
Results may differ from a plain program's by a relative error of at most 0.014.
Values may be sent and summed in bfloat16 or wider, within the bound.
A program may use at most 256 MiB of HBM per device.

v0:
```python
import jax
import jax.numpy as jnp
from jax import lax
from jax.sharding import PartitionSpec as P

QUERY_HEADS = 15
KEY_VALUE_HEADS = 5
HEAD_SIZE = 64


def layout(lengths_row, token_rows):
    seq_ends = jnp.cumsum(lengths_row)
    positions = jnp.arange(token_rows, dtype=jnp.int32)
    passed = positions[:, None] >= seq_ends[None, :]
    segment = jnp.sum(passed.astype(jnp.int32), axis=1)
    seq_start = jnp.sum(jnp.where(passed, lengths_row[None, :], 0), axis=1)
    offset = (positions - seq_start).astype(jnp.float32)
    living = positions < seq_ends[-1]
    allowed = (
        (segment[:, None] == segment[None, :])
        & (positions[None, :] <= positions[:, None])
        & living[:, None]
    )
    allowed = allowed | (positions[:, None] == positions[None, :])
    return (offset, living.astype(jnp.float32), allowed)


def rotation(offset, half_dim):
    frequency = 10000.0 ** (-jnp.arange(half_dim, dtype=jnp.float32) / half_dim)
    angles = offset[:, None] * frequency[None, :]
    return (jnp.cos(angles)[:, None, :], jnp.sin(angles)[:, None, :])


def apply_rotary(values, cosine_table, sine_table):
    half_dim = values.shape[-1] // 2
    leading = values[..., :half_dim]
    trailing = values[..., half_dim:]
    return jnp.concatenate(
        [
            leading * cosine_table - trailing * sine_table,
            trailing * cosine_table + leading * sine_table,
        ],
        axis=-1,
    )


def reverse_rotary(gradient, cosine_table, sine_table):
    half_dim = gradient.shape[-1] // 2
    leading = gradient[..., :half_dim]
    trailing = gradient[..., half_dim:]
    return jnp.concatenate(
        [
            leading * cosine_table + trailing * sine_table,
            trailing * cosine_table - leading * sine_table,
        ],
        axis=-1,
    )


def rms_scale(values):
    return lax.rsqrt(jnp.mean(values * values, axis=-1, keepdims=True) + 1e-05)


def matrix_product(left, right):
    return jnp.dot(left, right, preferred_element_type=jnp.float32)


def rows_outer(left, right):
    return jnp.einsum("ra,rb->ab", left, right, preferred_element_type=jnp.float32)


def multiply_by_transpose(left, right):
    return jnp.einsum("rb,ab->ra", left, right, preferred_element_type=jnp.float32)


def norm_back(grad_unit, unit, scale):
    return scale * (grad_unit - unit * jnp.mean(grad_unit * unit, axis=-1, keepdims=True))


def body(
    tokens,
    cotangent,
    seq_lengths,
    w_query,
    key_weight,
    value_weight,
    w_out,
    w_gate,
    w_up,
    w_down,
    gain_attn,
    gain_ffn,
):
    token_rows = tokens.shape[0]
    shard_group = QUERY_HEADS // KEY_VALUE_HEADS
    offset, living, allowed = layout(seq_lengths[0], token_rows)
    cosine_table, sine_table = rotation(offset, HEAD_SIZE // 2)
    live_col = living[:, None]
    gathered = (
        lax.all_gather(w_query, "shard", axis=0, tiled=True),
        lax.all_gather(key_weight, "shard", axis=0, tiled=True),
        lax.all_gather(value_weight, "shard", axis=0, tiled=True),
        lax.all_gather(w_out, "shard", axis=0, tiled=True),
        lax.all_gather(w_gate, "shard", axis=0, tiled=True),
        lax.all_gather(w_up, "shard", axis=0, tiled=True),
        lax.all_gather(w_down, "shard", axis=0, tiled=True),
        lax.all_gather(gain_attn, "shard", axis=0, tiled=True),
        lax.all_gather(gain_ffn, "shard", axis=0, tiled=True),
    )
    (
        full_query,
        complete_key,
        complete_value,
        full_out,
        full_gate,
        full_up,
        full_down,
        full_gain_attn,
        full_gain_ffn,
    ) = gathered
    masked = tokens.astype(jnp.float32) * live_col
    scale_one = rms_scale(masked)
    unit_one = masked * scale_one
    normalized_input = (unit_one * full_gain_attn.astype(jnp.float32)).astype(jnp.bfloat16)
    query_rows = matrix_product(normalized_input, full_query).reshape(
        token_rows, QUERY_HEADS, HEAD_SIZE
    )
    unrotated_keys = matrix_product(normalized_input, complete_key).reshape(
        token_rows, KEY_VALUE_HEADS, HEAD_SIZE
    )
    projected_values = matrix_product(normalized_input, complete_value).reshape(
        token_rows, KEY_VALUE_HEADS, HEAD_SIZE
    )
    rotated_query = (
        apply_rotary(query_rows, cosine_table, sine_table)
        .astype(jnp.bfloat16)
        .reshape(token_rows, KEY_VALUE_HEADS, shard_group, HEAD_SIZE)
    )
    k_rot = apply_rotary(unrotated_keys, cosine_table, sine_table).astype(jnp.bfloat16)
    v_low = projected_values.astype(jnp.bfloat16)
    scores = (
        jnp.einsum("ikgd,jkd->kgij", rotated_query, k_rot, preferred_element_type=jnp.float32)
        * 0.125
    )
    shifted = jnp.where(allowed, scores, -1e30)
    peak = jnp.max(shifted, axis=-1, keepdims=True)
    raised = jnp.exp(shifted - peak)
    row_total = jnp.sum(raised, axis=-1, keepdims=True)
    probs = raised / row_total
    log_total = peak + jnp.log(row_total)
    attended = jnp.einsum(
        "kgij,jkd->ikgd", probs.astype(jnp.bfloat16), v_low, preferred_element_type=jnp.float32
    )
    attn_low = attended.reshape(token_rows, QUERY_HEADS * HEAD_SIZE).astype(jnp.bfloat16)
    middle = masked + matrix_product(attn_low, full_out)
    scale_two = rms_scale(middle)
    unit_two = middle * scale_two
    normed_two = (unit_two * full_gain_ffn.astype(jnp.float32)).astype(jnp.bfloat16)
    gate = matrix_product(normed_two, full_gate)
    up_proj = matrix_product(normed_two, full_up)
    sigmoid_gate = jax.nn.sigmoid(gate)
    silu_gate = gate * sigmoid_gate
    hidden = (silu_gate * up_proj).astype(jnp.bfloat16)
    ffn_out = matrix_product(hidden, full_down)
    output = (live_col * (middle + ffn_out)).astype(jnp.bfloat16)
    again = (
        lax.all_gather(w_query, "shard", axis=0, tiled=True),
        lax.all_gather(key_weight, "shard", axis=0, tiled=True),
        lax.all_gather(value_weight, "shard", axis=0, tiled=True),
        lax.all_gather(w_out, "shard", axis=0, tiled=True),
        lax.all_gather(w_gate, "shard", axis=0, tiled=True),
        lax.all_gather(w_up, "shard", axis=0, tiled=True),
        lax.all_gather(w_down, "shard", axis=0, tiled=True),
        lax.all_gather(gain_attn, "shard", axis=0, tiled=True),
        lax.all_gather(gain_ffn, "shard", axis=0, tiled=True),
    )
    (
        back_query,
        back_key,
        back_value,
        output_backward,
        back_gate,
        back_up,
        back_down,
        back_gain_attn,
        back_gain_ffn,
    ) = again
    grad_rows = cotangent.astype(jnp.float32) * live_col
    grad_ffn = grad_rows.astype(jnp.bfloat16)
    grad_down_w = rows_outer(hidden, grad_ffn)
    grad_hidden = multiply_by_transpose(grad_ffn, back_down)
    grad_gate_low = (
        grad_hidden * up_proj * sigmoid_gate * (1.0 + gate * (1.0 - sigmoid_gate))
    ).astype(jnp.bfloat16)
    grad_up_low = (grad_hidden * silu_gate).astype(jnp.bfloat16)
    grad_gate_w = rows_outer(normed_two, grad_gate_low)
    grad_up_w = rows_outer(normed_two, grad_up_low)
    grad_normed_two = multiply_by_transpose(grad_gate_low, back_gate) + multiply_by_transpose(
        grad_up_low, back_up
    )
    grad_gain_two = jnp.sum(grad_normed_two * unit_two, axis=0)
    grad_middle = grad_rows + norm_back(
        grad_normed_two * back_gain_ffn.astype(jnp.float32), unit_two, scale_two
    )
    attention_gradient_reduced = grad_middle.astype(jnp.bfloat16)
    grad_out_w = rows_outer(attn_low, attention_gradient_reduced)
    grad_attended = (
        multiply_by_transpose(attention_gradient_reduced, output_backward)
        .astype(jnp.bfloat16)
        .reshape(token_rows, KEY_VALUE_HEADS, shard_group, HEAD_SIZE)
    )
    scores_again = (
        jnp.einsum("ikgd,jkd->kgij", rotated_query, k_rot, preferred_element_type=jnp.float32)
        * 0.125
    )
    probs_again = jnp.exp(jnp.where(allowed, scores_again, -1e30) - log_total)
    probs_low = probs_again.astype(jnp.bfloat16)
    grad_probs = jnp.einsum(
        "ikgd,jkd->kgij", grad_attended, v_low, preferred_element_type=jnp.float32
    )
    row_delta = jnp.sum(probs_again * grad_probs, axis=-1, keepdims=True)
    grad_scores = (probs_again * (grad_probs - row_delta)).astype(jnp.bfloat16)
    grad_q_rot = (
        jnp.einsum("kgij,jkd->ikgd", grad_scores, k_rot, preferred_element_type=jnp.float32) * 0.125
    ).reshape(token_rows, QUERY_HEADS, HEAD_SIZE)
    rotated_key_gradient = (
        jnp.einsum("kgij,ikgd->jkd", grad_scores, rotated_query, preferred_element_type=jnp.float32)
        * 0.125
    )
    value_gradients = jnp.einsum(
        "kgij,ikgd->jkd", probs_low, grad_attended, preferred_element_type=jnp.float32
    )
    grad_queries = (
        reverse_rotary(grad_q_rot, cosine_table, sine_table)
        .astype(jnp.bfloat16)
        .reshape(token_rows, QUERY_HEADS * HEAD_SIZE)
    )
    grad_keys = (
        reverse_rotary(rotated_key_gradient, cosine_table, sine_table)
        .astype(jnp.bfloat16)
        .reshape(token_rows, KEY_VALUE_HEADS * HEAD_SIZE)
    )
    value_gradients_reduced = value_gradients.astype(jnp.bfloat16).reshape(
        token_rows, KEY_VALUE_HEADS * HEAD_SIZE
    )
    grad_query_w = rows_outer(normalized_input, grad_queries)
    grad_key_w = rows_outer(normalized_input, grad_keys)
    grad_value_w = rows_outer(normalized_input, value_gradients_reduced)
    grad_normed = (
        multiply_by_transpose(grad_queries, back_query)
        + multiply_by_transpose(grad_keys, back_key)
        + multiply_by_transpose(value_gradients_reduced, back_value)
    )
    grad_gain_one = jnp.sum(grad_normed * unit_one, axis=0)
    grad_input = live_col * (
        grad_middle
        + norm_back(grad_normed * back_gain_attn.astype(jnp.float32), unit_one, scale_one)
    )
    grad_tokens = grad_input.astype(jnp.bfloat16)
    owned = (
        lax.psum_scatter(grad_query_w, "shard", scatter_dimension=0, tiled=True),
        lax.psum_scatter(grad_key_w, "shard", scatter_dimension=0, tiled=True),
        lax.psum_scatter(grad_value_w, "shard", scatter_dimension=0, tiled=True),
        lax.psum_scatter(grad_out_w, "shard", scatter_dimension=0, tiled=True),
        lax.psum_scatter(grad_gate_w, "shard", scatter_dimension=0, tiled=True),
        lax.psum_scatter(grad_up_w, "shard", scatter_dimension=0, tiled=True),
        lax.psum_scatter(grad_down_w, "shard", scatter_dimension=0, tiled=True),
        lax.psum_scatter(grad_gain_one, "shard", scatter_dimension=0, tiled=True),
        lax.psum_scatter(grad_gain_two, "shard", scatter_dimension=0, tiled=True),
    )
    summed = lax.psum(
        (owned[0], owned[1], owned[2], owned[3], owned[4], owned[5], owned[6], owned[7], owned[8]),
        "replica",
    )
    return (
        output,
        grad_tokens,
        summed[0],
        summed[1],
        summed[2],
        summed[3],
        summed[4],
        summed[5],
        summed[6],
        summed[7],
        summed[8],
    )


def solution(mesh):
    return jax.shard_map(
        body,
        mesh=mesh,
        in_specs=(
            P(("replica", "shard"), None),
            P(("replica", "shard"), None),
            P(("replica", "shard"), None),
            P("shard", None),
            P("shard", None),
            P("shard", None),
            P("shard", None),
            P("shard", None),
            P("shard", None),
            P("shard", None),
            P("shard"),
            P("shard"),
        ),
        out_specs=(
            P(("replica", "shard"), None),
            P(("replica", "shard"), None),
            P("shard", None),
            P("shard", None),
            P("shard", None),
            P("shard", None),
            P("shard", None),
            P("shard", None),
            P("shard", None),
            P("shard"),
            P("shard"),
        ),
        check_vma=False,
    )
```

profile of v0, /device:TPU:0, one launch (start us, length us, event | category | flops | bytes accessed | tf_op | source)
XLA Modules:
  0.0 986.6 jit_solution(12190872079346372931)
XLA Ops:
  13.4 1.3 fusion.47
  17.1 18.5 %all-reduce.10 = (bf16[960]{0:T(1024)(128)(2,1)S(1)}, bf16[960]{0:T(1024)(128)(2,1)S(1)}) all-reduce(bf16[960]{0:T(1024)(128)(2,1)S(1)} %dynamic-update-slice, bf16[960]{0:T(1024)(128)(2,1)S(1)} %dynamic-update-slice.1), channel_id=1, replica_groups=mesh['replica'=4,'shard'=8] {'shard'}, use_global_device_ids=true, to_apply=%add | all-reduce | flops 1920 | bytes 7680
  36.2 15.4 %all-gather.1 = bf16[8,120,320]{1,2,0:T(8,128)(2,1)S(1)} all-gather(bf16[1,120,320]{1,2,0:T(8,128)(2,1)S(1)} %bitcast.145), channel_id=1, replica_groups=mesh['replica'=4,'shard'=8] {'shard'}, dimensions={0}, use_global_device_ids=true | all-gather | bytes 691200 | tf_op jit(solution)/shard_map/all_gather | solution.py:101
  52.6 17.9 %all-gather = bf16[8,120,320]{1,2,0:T(8,128)(2,1)S(1)} all-gather(bf16[1,120,320]{1,2,0:T(8,128)(2,1)S(1)} %bitcast.146), channel_id=1, replica_groups=mesh['replica'=4,'shard'=8] {'shard'}, dimensions={0}, use_global_device_ids=true | all-gather | bytes 691200 | tf_op jit(solution)/shard_map/all_gather | solution.py:102
  71.5 1.6 convolution_convert_fusion.1
  75.0 3.6 fusion.45
  79.1 15.1 %fusion.9 = (f32[5,3,768]{2,1,0:T(4,128)S(1)}, f32[5,768,768,3]{2,1,3,0:T(8,128)}) fusion(pred[768,768]{0,1:T(8,128)(4,1)S(1)} %fusion.16, bf16[768,5,3,32]{0,3,2,1:T(8,128)(2,1)S(1)} %bitcast.131, bf16[768,5,3,32]{0,3,2,1:T(8,128)(2,1)S(1)} %bitcast.129, bf16[768,5,32]{0,2,1:T(8,128)(2,1)S(1)} %get-tuple-element.42, ...), kind=kOutput, calls=%fused_computation.14 | convolution fusion | flops 1162924800 | bytes 37991424 | tf_op jit(solution)/shard_map/ikgd,jkd->kgij/dot_general | solution.py:142
  94.2 15.7 %fusion.3 = f32[5,3,768]{2,1,0:T(4,128)S(1)} fusion(f32[5,3,768]{2,1,0:T(4,128)S(1)} %get-tuple-element.47, f32[5,768,768,3]{2,1,3,0:T(8,128)} %get-tuple-element.48, pred[768,768]{0,1:T(8,128)(4,1)S(1)} %fusion.16), kind=kLoop, calls=%fused_computation.9 | loop fusion | flops 35377920 | bytes 36071424 | tf_op jit(solution)/shard_map/reduce_sum | solution.py:148
  110.0 17.1 %fusion.17 = bf16[5,64,3,768]{3,1,2,0:T(8,128)(2,1)} fusion(bf16[768,5,64,1]{0,2,3,1:T(8,128)(2,1)S(1)} %bitcast.142, f32[5,3,768]{2,1,0:T(4,128)S(1)} %fusion.3, f32[5,3,768]{2,1,0:T(4,128)S(1)} %get-tuple-element.47, f32[5,768,768,3]{2,1,3,0:T(8,128)} %get-tuple-element.48, pred[768,768]{0,1:T(8,128)(4,1)S(1)} %fusion.16), kind=kOutput, calls=%fused_computation.43 | convolution fusion | flops 1177436160 | bytes 38037504 | tf_op jit(solution)/shard_map/kgij,jkd->ikgd/dot_general | solution.py:151
  127.1 4.0 multiply_reduce_fusion.4
  134.2 9.3 fusion.49
  143.5 40.9 %all-gather.12.cloned.1.call-done = bf16[960,2560]{1,0:T(8,128)(2,1)} async-done(((bf16[120,2560]{1,0:T(8,128)(2,1)}), bf16[960,2560]{1,0:T(8,128)(2,1)}) %all-gather.12.cloned.1.call-update) | async-done | bytes 4915216 | tf_op jit(solution)/shard_map/all_gather | solution.py:104
  184.3 10.4 %fusion.48 = f32[768,2560]{1,0:T(8,128)} fusion(bf16[768,960]{0,1:T(8,128)(2,1)} %copy-done.17, bf16[960,2560]{1,0:T(8,128)(2,1)} %all-gather.12.cloned.1.call-done), kind=kOutput, calls=%fused_computation.99 | convolution fusion | flops 3774873600 | bytes 14254080 | tf_op jit(solution)/shard_map/dot_general | solution.py:65
  194.7 46.0 %all-gather.16.cloned.1.call-done = bf16[2560,960]{1,0:T(8,128)(2,1)} async-done(((bf16[320,960]{1,0:T(8,128)(2,1)}), bf16[2560,960]{1,0:T(8,128)(2,1)}) %all-gather.16.cloned.1.call-update) | async-done | bytes 4915216 | tf_op jit(solution)/shard_map/all_gather | solution.py:106
  240.7 15.0 %multiply_convert_fusion = (bf16[768,2560]{1,0:T(8,128)(2,1)}, bf16[768,2560]{1,0:T(8,128)(2,1)}, bf16[768,2560]{1,0:T(8,128)(2,1)}) fusion(f32[768,2560]{1,0:T(8,128)} %fusion.48, f32[768,2560]{1,0:T(8,128)} %fusion.49, bf16[2560,960]{1,0:T(8,128)(2,1)} %all-gather.16.cloned.1.call-done, bf16[768,960]{0,1:T(8,128)(2,1)S(1)} %copy-done.16, f32[768]{0:T(1024)S(1)} %fusion.34), kind=kOutput, calls=%fused_computation.15 | convolution fusion | flops 3806576640 | bytes 33917952 | tf_op jit(solution)/shard_map/rb,ab->ra/dot_general | solution.py:73
  255.7 6.3 fusion.50
  262.0 6.9 multiply_reduce_fusion
  270.4 1.7 convolution_convert_fusion
  272.1 15.5 %fusion.27 = bf16[5,64,768]{2,1,0:T(8,128)(2,1)} fusion(bf16[768,5,3,64]{0,3,2,1:T(8,128)(2,1)S(1)} %bitcast.136, f32[5,3,768]{2,1,0:T(4,128)} %log_add_fusion, f32[5,768,768,3]{2,1,3,0:T(8,128)} %get-tuple-element.48, pred[768,768]{0,1:T(8,128)(4,1)S(1)} %fusion.16), kind=kOutput, calls=%fused_computation.59 | convolution fusion | flops 1168097280 | bytes 37991424 | tf_op jit(solution)/shard_map/kgij,ikgd->jkd/dot_general | solution.py:230
  287.6 28.2 %fusion = (f32[5,3,768]{2,1,0:T(4,128)S(1)}, f32[5,768,768,3]{2,1,3,0:T(8,128)}) fusion(f32[5,3,768]{2,1,0:T(4,128)} %log_add_fusion, f32[5,768,768,3]{2,1,3,0:T(8,128)} %get-tuple-element.48, pred[768,768]{0,1:T(8,128)(4,1)S(1)} %fusion.16, bf16[768,5,64,1]{0,2,3,1:T(8,128)(2,1)} %bitcast.141, bf16[768,5,3,64]{0,3,2,1:T(8,128)(2,1)S(1)} %bitcast.137), kind=kOutput, calls=%fused_computation.2 | convolution fusion | flops 1176687360 | bytes 73426944 | tf_op jit(solution)/shard_map/ikgd,jkd->kgij/dot_general | solution.py:218
  315.9 1.9 fusion.42
  317.8 29.9 %fusion.2 = bf16[5,3,768,768]{2,3,1,0:T(8,128)(2,1)} fusion(f32[5,768,768,3]{2,1,3,0:T(8,128)} %get-tuple-element.53, f32[5,3,768]{2,1,0:T(4,128)S(1)} %get-tuple-element.52, f32[5,3,768]{2,1,0:T(4,128)S(1)} %copy-done.27, f32[5,768,768,3]{2,1,3,0:T(8,128)} %get-tuple-element.48, pred[768,768]{0,1:T(8,128)(4,1)S(1)} %fusion.16), kind=kLoop, calls=%fused_computation.4 | loop fusion | flops 53084160 | bytes 89155584 | tf_op jit(solution)/shard_map/convert_element_type | solution.py:222
  347.8 11.7 %fusion.22 = f32[768,5,64]{0,2,1:T(8,128)S(1)} fusion(bf16[5,3,768,768]{2,3,1,0:T(8,128)(2,1)} %fusion.2, bf16[768,5,3,32]{0,3,2,1:T(8,128)(2,1)} %bitcast.132, bf16[768,5,3,32]{0,3,2,1:T(8,128)(2,1)S(1)} %bitcast.130), kind=kOutput, calls=%fused_computation.55 | convolution fusion | flops 1135656960 | bytes 20152320 | tf_op jit(solution)/shard_map/kgij,ikgd->jkd/dot_general | solution.py:227
  359.7 1.9 fusion.43
  361.6 5.9 fusion.31
  368.6 9.3 convolution_multiply_fusion
  379.6 3.7 fusion.44
  383.4 10.2 %fusion.53 = f32[960,2560]{1,0:T(8,128)} fusion(bf16[768,960]{0,1:T(8,128)(2,1)} %copy-done.17, bf16[768,2560]{1,0:T(8,128)(2,1)} %get-tuple-element.32), kind=kOutput, calls=%fused_computation.104 | convolution fusion | flops 3774873600 | bytes 15237120 | tf_op jit(solution)/shard_map/ra,rb->ab/dot_general | solution.py:69
  393.7 10.4 %fusion.52 = f32[960,2560]{1,0:T(8,128)} fusion(bf16[768,960]{0,1:T(8,128)(2,1)} %copy-done.17, bf16[768,2560]{1,0:T(8,128)(2,1)} %get-tuple-element.33), kind=kOutput, calls=%fused_computation.103 | convolution fusion | flops 3774873600 | bytes 15237120 | tf_op jit(solution)/shard_map/ra,rb->ab/dot_general | solution.py:69
  404.6 10.9 %fusion.23 = f32[2560,960]{1,0:T(8,128)} fusion(bf16[768,2560]{1,0:T(8,128)(2,1)} %get-tuple-element.34, bf16[768,960]{0,1:T(8,128)(2,1)} %param.13, f32[768]{0:T(1024)S(1)} %fusion.34), kind=kOutput, calls=%fused_computation.56 | convolution fusion | flops 3777085440 | bytes 15240192 | tf_op jit(solution)/shard_map/ra,rb->ab/dot_general | solution.py:69
  416.4 13.7 %all-reduce.14.cloned.1.call-done = (f32[960,320]{0,1:T(8,128)}, f32[960,320]{0,1:T(8,128)}) async-done(((f32[960,320]{0,1:T(8,128)}, f32[960,320]{0,1:T(8,128)}), (f32[960,320]{0,1:T(8,128)}, f32[960,320]{0,1:T(8,128)})) %all-reduce.14.cloned.1.call-update) | async-done | bytes 2457616
  430.1 1.9 constant_dynamic-slice_fusion
  432.0 46.9 %reduce-scatter.10.cloned.1.call-done = f32[120,960]{1,0:T(8,128)} async-done(((f32[960,960]{1,0:T(8,128)}), f32[120,960]{1,0:T(8,128)}) %reduce-scatter.10.cloned.1.call-update) | async-done | bytes 460816 | tf_op jit(solution)/shard_map/reduce_scatter | solution.py:264
  479.0 48.0 %reduce-scatter.8.cloned.1.call-done = f32[120,960]{1,0:T(8,128)} async-done(((f32[960,960]{1,0:T(8,128)}), f32[120,960]{1,0:T(8,128)}) %reduce-scatter.8.cloned.1.call-update) | async-done | bytes 460816 | tf_op jit(solution)/shard_map/reduce_scatter | solution.py:261
  527.0 103.7 %reduce-scatter.14.cloned.1.call-done = f32[120,2560]{1,0:T(8,128)} async-done(((f32[960,2560]{1,0:T(8,128)}), f32[120,2560]{1,0:T(8,128)}) %reduce-scatter.14.cloned.1.call-update) | async-done | bytes 1228816 | tf_op jit(solution)/shard_map/reduce_scatter | solution.py:266
  630.7 103.9 %reduce-scatter.12.cloned.1.call-done = f32[120,2560]{1,0:T(8,128)} async-done(((f32[960,2560]{1,0:T(8,128)}), f32[120,2560]{1,0:T(8,128)}) %reduce-scatter.12.cloned.1.call-update) | async-done | bytes 1228816 | tf_op jit(solution)/shard_map/reduce_scatter | solution.py:265
  734.6 110.1 %reduce-scatter.16.cloned.1.call-done = f32[320,960]{1,0:T(8,128)} async-done(((f32[2560,960]{1,0:T(8,128)}), f32[320,960]{1,0:T(8,128)}) %reduce-scatter.16.cloned.1.call-update) | async-done | bytes 1228816 | tf_op jit(solution)/shard_map/reduce_scatter | solution.py:267
  846.8 1.7 fusion.54
  848.5 3.3 multiply_reduce_fusion.1
  851.8 13.9 %all-reduce.6 = (f32[960]{0:T(1024)S(1)}, f32[960]{0:T(1024)S(1)}) all-reduce(f32[960]{0:T(1024)S(1)} %get-tuple-element.13, f32[960]{0:T(1024)S(1)} %get-tuple-element.11), channel_id=9, replica_groups=mesh['replica'=4,'shard'=8] {'shard'}, use_global_device_ids=true, to_apply=%region_25.26.clone | all-reduce | flops 1920 | bytes 15360
  865.9 10.8 %all-reduce.8 = (f32[120]{0:T(128)}, f32[120]{0:T(128)}) all-reduce(f32[120]{0:T(128)S(1)} %dynamic-slice.7, f32[120]{0:T(128)S(1)} %dynamic-slice.9), channel_id=1, replica_groups=mesh['replica'=4,'shard'=8] {'replica'}, use_global_device_ids=true, to_apply=%region_26.27 | all-reduce | flops 240 | bytes 1920 | tf_op jit(solution)/shard_map/psum | solution.py:271
  876.7 5.0 multiply_convert_fusion.3
  881.7 7.9 multiply_convert_fusion.4
  889.6 79.7 %all-reduce.16.cloned.1.call-done = (f32[120,960]{1,0:T(8,128)}, f32[120,320]{0,1:T(8,128)}, f32[120,320]{0,1:T(8,128)}, f32[120,960]{1,0:T(8,128)}, f32[120,256...) async-done(((f32[120,960]{1,0:T(8,128)}, f32[120,320]{0,1:T(8,128)}, f32[120,320]{0,1:T(8,128)}, f32[120,960]{1,0:T(8,128)}, f32[120,2560]{1,0:T(8,128)}, ...) | async-done | bytes 4915216 | tf_op jit(solution)/shard_map/psum | solution.py:271
  969.3 2.0 copy.68
  971.3 1.6 copy.69
  972.9 1.6 copy.70
  974.5 2.0 copy.71
  (153 shorter events, 26.1 us)
Async XLA Ops:
  7.2 28.9 %copy-start.37 = (s32[1,4]{1,0:T(1,128)S(1)}, s32[1,4]{1,0:T(1,128)}, u32[]{:S(2)}) copy-start(s32[1,4]{1,0:T(1,128)} %param.14) | copy-start | bytes 52
  7.2 28.4 %copy-start = (bf16[768,960]{0,1:T(8,128)(2,1)S(1)}, bf16[768,960]{0,1:T(8,128)(2,1)}, u32[]{:S(2)}) copy-start(bf16[768,960]{0,1:T(8,128)(2,1)} %param.12) | copy-start | bytes 4423684
  7.2 29.0 %copy-start.31 = (bf16[120,320]{0,1:T(8,128)(2,1)S(1)}, bf16[120,320]{0,1:T(8,128)(2,1)}, u32[]{:S(2)}) copy-start(bf16[120,320]{0,1:T(8,128)(2,1)} %param.16) | copy-start | bytes 230404
  7.2 67.8 %all-gather.8.cloned.1.call-start = ((), (), s32[]{:S(2)}) async-start(), calls=%async_computation.5 | async-start | bytes 2211840 | tf_op jit(solution)/shard_map/all_gather | solution.py:100
  7.9 119.1 %all-gather.10.cloned.1.call-start = ((), (), s32[]{:S(2)}) async-start(), calls=%async_computation.6 | async-start | bytes 2211840 | tf_op jit(solution)/shard_map/all_gather | solution.py:103
  8.7 124.4 %all-gather.14.cloned.1.call-start = ((), (), s32[]{:S(2)}) async-start(), calls=%async_computation.8 | async-start | bytes 5529600 | tf_op jit(solution)/shard_map/all_gather | solution.py:105
  9.4 174.9 %all-gather.12.cloned.1.call-start = ((), (), s32[]{:S(2)}) async-start(), calls=%async_computation.7 | async-start | bytes 5529600 | tf_op jit(solution)/shard_map/all_gather | solution.py:104
  10.0 42.6 %copy-start.32 = (bf16[120,320]{0,1:T(8,128)(2,1)S(1)}, bf16[120,320]{0,1:T(8,128)(2,1)}, u32[]{:S(2)}) copy-start(bf16[120,320]{0,1:T(8,128)(2,1)} %param.17) | copy-start | bytes 230404
  10.0 230.7 %all-gather.16.cloned.1.call-start = ((), (), s32[]{:S(2)}) async-start(), calls=%async_computation.9 | async-start | bytes 5898240 | tf_op jit(solution)/shard_map/all_gather | solution.py:106
  10.6 419.5 %all-reduce.14.cloned.1.call-start = ((), (), s32[]{:S(2)}) async-start(), calls=%async_computation.15 | async-start | bytes 5242880
  35.6 39.4 %copy-start.33 = (f32[960]{0:T(1024)}, f32[960]{0:T(1024)S(1)}, u32[]{:S(2)}) copy-start(f32[960]{0:T(1024)S(1)} %convert_element_type.106) | copy-start | bytes 11524
  36.0 38.9 %copy-start.35 = (f32[768]{0:T(1024)}, f32[768]{0:T(1024)S(1)}, u32[]{:S(2)}) copy-start(f32[768]{0:T(1024)S(1)} %add_rsqrt_fusion.1) | copy-start | bytes 9220
  52.6 20.5 %copy-start.8 = (bf16[960,320]{0,1:T(8,128)(2,1)}, bf16[960,320]{0,1:T(8,128)(2,1)S(1)}, u32[]{:S(2)}) copy-start(bf16[960,320]{0,1:T(8,128)(2,1)S(1)} %reshape.182) | copy-start | bytes 1843204
  71.5 2.4 copy-start.10
  74.3 4.3 copy-start.12
  74.3 4.3 copy-start.14
  74.9 4.1 copy-start.23
  74.9 4.1 copy-start.25
  79.0 15.2 %copy-start.5 = (bf16[768,15,32]{0,2,1:T(8,128)(2,1)}, bf16[768,15,32]{0,2,1:T(8,128)(2,1)S(1)}, u32[]{:S(2)}) copy-start(bf16[768,15,32]{0,2,1:T(8,128)(2,1)S(1)} %get-tuple-element.37) | copy-start | bytes 2211844
  79.0 15.2 %copy-start.7 = (bf16[768,15,32]{0,2,1:T(8,128)(2,1)}, bf16[768,15,32]{0,2,1:T(8,128)(2,1)S(1)}, u32[]{:S(2)}) copy-start(bf16[768,15,32]{0,2,1:T(8,128)(2,1)S(1)} %get-tuple-element.38) | copy-start | bytes 2211844
  94.2 15.7 %copy-start.28 = (bf16[768,320]{0,1:T(8,128)(2,1)S(1)}, bf16[768,320]{0,1:T(8,128)(2,1)}, u32[]{:S(2)}) copy-start(bf16[768,320]{0,1:T(8,128)(2,1)} %convolution_convert_fusion.1) | copy-start | bytes 1474564
  143.4 97.2 %copy-start.16 = (bf16[768,960]{0,1:T(8,128)(2,1)S(1)}, bf16[768,960]{0,1:T(8,128)(2,1)}, u32[]{:S(2)}) copy-start(bf16[768,960]{0,1:T(8,128)(2,1)} %param.13) | copy-start | bytes 4423684
  240.7 15.0 %copy-start.38 = (bf16[960,2560]{1,0:T(8,128)(2,1)S(1)}, bf16[960,2560]{1,0:T(8,128)(2,1)}, u32[]{:S(2)}) copy-start(bf16[960,2560]{1,0:T(8,128)(2,1)} %all-gather.12.cloned.1.call-done) | copy-start | bytes 14745604
  255.7 6.3 copy-start.2
  255.7 6.3 copy-start.41
  270.4 1.7 copy-start.4
  287.6 28.2 %copy-start.29 = (bf16[5,64,768]{2,1,0:T(8,128)(2,1)S(1)}, bf16[5,64,768]{2,1,0:T(8,128)(2,1)}, u32[]{:S(2)}) copy-start(bf16[5,64,768]{2,1,0:T(8,128)(2,1)} %fusion.27) | copy-start | bytes 1474564
  287.6 28.2 %copy-start.34 = (f32[960]{0:T(1024)S(1)}, f32[960]{0:T(1024)}, u32[]{:S(2)}) copy-start(f32[960]{0:T(1024)} %copy-done.33) | copy-start | bytes 11524
  287.6 28.3 %copy-start.36 = (f32[768]{0:T(1024)S(1)}, f32[768]{0:T(1024)}, u32[]{:S(2)}) copy-start(f32[768]{0:T(1024)} %copy-done.35) | copy-start | bytes 9220
  315.9 2.0 copy-start.27
  317.8 30.0 %copy-start.6 = (bf16[768,15,32]{0,2,1:T(8,128)(2,1)S(1)}, bf16[768,15,32]{0,2,1:T(8,128)(2,1)}, u32[]{:S(2)}) copy-start(bf16[768,15,32]{0,2,1:T(8,128)(2,1)} %copy-done.5) | copy-start | bytes 2211844
  347.8 11.8 %copy-start.13 = (f32[768,32]{0,1:T(8,128)S(1)}, f32[768,32]{0,1:T(8,128)}, u32[]{:S(2)}) copy-start(f32[768,32]{0,1:T(8,128)} %copy-done.12) | copy-start | bytes 294916
  347.8 11.8 %copy-start.15 = (f32[768,32]{0,1:T(8,128)S(1)}, f32[768,32]{0,1:T(8,128)}, u32[]{:S(2)}) copy-start(f32[768,32]{0,1:T(8,128)} %copy-done.14) | copy-start | bytes 294916
  361.6 117.4 %reduce-scatter.10.cloned.1.call-start = ((), (), s32[]{:S(2)}) async-start(), calls=%async_computation.11 | async-start | bytes 4423680 | tf_op jit(solution)/shard_map/reduce_scatter | solution.py:264
  367.6 159.4 %reduce-scatter.8.cloned.1.call-start = ((), (), s32[]{:S(2)}) async-start(), calls=%async_computation.10 | async-start | bytes 4423680 | tf_op jit(solution)/shard_map/reduce_scatter | solution.py:261
  383.4 247.4 %reduce-scatter.14.cloned.1.call-start = ((), (), s32[]{:S(2)}) async-start(), calls=%async_computation.13 | async-start | bytes 11059200 | tf_op jit(solution)/shard_map/reduce_scatter | solution.py:266
  393.7 341.0 %reduce-scatter.12.cloned.1.call-start = ((), (), s32[]{:S(2)}) async-start(), calls=%async_computation.12 | async-start | bytes 11059200 | tf_op jit(solution)/shard_map/reduce_scatter | solution.py:265
  404.1 440.6 %reduce-scatter.16.cloned.1.call-start = ((), (), s32[]{:S(2)}) async-start(), calls=%async_computation.14 | async-start | bytes 11796480 | tf_op jit(solution)/shard_map/reduce_scatter | solution.py:267
  415.6 429.2 %copy-start.9 = (bf16[960,320]{0,1:T(8,128)(2,1)S(1)}, bf16[960,320]{0,1:T(8,128)(2,1)}, u32[]{:S(2)}) copy-start(bf16[960,320]{0,1:T(8,128)(2,1)} %copy-done.8) | copy-start | bytes 1843204
  415.6 553.7 %all-reduce.16.cloned.1.call-start = ((), (), s32[]{:S(2)}) async-start(), calls=%async_computation.16 | async-start | bytes 10158080 | tf_op jit(solution)/shard_map/psum | solution.py:271
  844.8 2.0 copy-start.39
  846.8 1.7 copy-start.11
  846.8 1.7 copy-start.30
  876.7 5.0 copy-start.3
  876.7 5.0 copy-start.42
  969.3 7.2 copy-start.22
  969.3 8.2 copy-start.21
  974.5 4.0 copy-start.20
  (7 other events, 8.8 us)
Sparse Core Ops, SparseCore 0:
  9.7 32.9 all-gather.7
  44.3 31.7 all-gather.9
  77.8 52.8 all-gather.13
  132.2 52.1 all-gather.11
  185.8 54.8 all-gather.15
  361.7 68.3 all-reduce.13
  432.4 46.5 reduce-scatter.9
  481.3 45.6 reduce-scatter.7
  529.3 101.3 reduce-scatter.13
  633.0 101.5 reduce-scatter.11
  736.9 107.7 reduce-scatter.15
  849.8 119.4 all-reduce.15
where the time goes:
time: 994 us; the launch traced here: 987 us
  waiting for transfers between devices  596 us (60%)
  matrix products  215 us (22%)
  blocking collectives  76.5 us (8%)
  other arithmetic  57.4 us (6%)
  local copies, waits for them, and re-layouts  23.5 us (2%)
  between operations  16.5 us (2%)
    reduce_scatter x1, waiting for transfers between devices, body(): lax.psum_scatter(grad_down_w, 'shard', scatter_dimension=0, tiled=True)  110 us
    reduce_scatter x1, waiting for transfers between devices, body(): lax.psum_scatter(grad_gate_w, 'shard', scatter_dimension=0, tiled=True)  104 us
    reduce_scatter x1, waiting for transfers between devices, body(): lax.psum_scatter(grad_up_w, 'shard', scatter_dimension=0, tiled=True)  104 us
    psum x1, waiting for transfers between devices, body(): lax.psum((owned[0], owned[1], owned[2], owned[3], owned[4], owned[5], own...  79.7 us
    reduce_scatter x1, waiting for transfers between devices, body(): lax.psum_scatter(grad_query_w, 'shard', scatter_dimension=0, tiled=True)  48 us
    reduce_scatter x1, waiting for transfers between devices, body(): lax.psum_scatter(grad_out_w, 'shard', scatter_dimension=0, tiled=True)  46.9 us
    all_gather x1, waiting for transfers between devices, body(): lax.all_gather(w_down, 'shard', axis=0, tiled=True)  46 us
    dot_general x7, matrix products, rows_outer(): jnp.einsum('ra,rb->ab', left, right, preferred_element_type=jnp.float32)  44.9 us
  transfers between devices with their start and end apart: 12, of which 9 were waited for; matrix products, arithmetic and copies ran while one was open for 16% of the time, Pallas kernels for 0%

commit v1 on v0

--- a/solution.py
+++ b/solution.py
@@ -6,6 +6,183 @@
 QUERY_HEADS = 15
 KEY_VALUE_HEADS = 5
 HEAD_SIZE = 64
+
+
+AXES = ("replica", "shard")
+
+
+def cells():
+    replicas = lax.axis_size("replica")
+    shards = lax.axis_size("shard")
+    return replicas, shards, lax.axis_index("replica"), lax.axis_index("shard")
+
+
+def swap(value, kind, bit):
+    replicas, shards, _, _ = cells()
+    pairs = []
+    for r in range(replicas):
+        for s in range(shards):
+            to = (r ^ bit) * shards + s if kind == "r" else r * shards + (s ^ bit)
+            pairs.append((r * shards + s, to))
+    return lax.ppermute(value, AXES, pairs)
+
+
+def my_bit(kind, bit):
+    _, _, r, s = cells()
+    return ((r if kind == "r" else s) // bit) % 2
+
+
+def bits_of(size):
+    found = []
+    bit = 1
+    while bit < size:
+        found.append(bit)
+        bit *= 2
+    return found
+
+
+def low(value):
+    return lax.reduce_precision(value.astype(jnp.float32), 8, 7).astype(jnp.bfloat16)
+
+
+class Spread:
+    def __init__(self, parts):
+        self.parts = parts
+
+    def axis(self, part):
+        return self.parts.index(part)
+
+
+def grow(value, spread, part):
+    axis = spread.axis(part)
+    other = swap(value, *part)
+    upper = my_bit(*part) == 1
+    first = jnp.where(upper, other, value)
+    second = jnp.where(upper, value, other)
+    return jnp.concatenate([first, second], axis=axis)
+
+
+def halve(value, spread, part):
+    axis = spread.axis(part)
+    upper = my_bit(*part) == 1
+    lower_half = lax.slice_in_dim(value, 0, 1, axis=axis)
+    upper_half = lax.slice_in_dim(value, 1, 2, axis=axis)
+    keep = jnp.where(upper, upper_half, lower_half)
+    send = jnp.where(upper, lower_half, upper_half)
+    other = swap(low(send), *part)
+    return keep.astype(jnp.float32) + other.astype(jnp.float32)
+
+
+def both(value, part):
+    mine = low(value)
+    return mine.astype(jnp.float32) + swap(mine, *part).astype(jnp.float32)
+
+
+def shard_parts():
+    _, shards, _, _ = cells()
+    return [("s", bit) for bit in reversed(bits_of(shards))]
+
+
+def replica_parts():
+    replicas, _, _, _ = cells()
+    return [("r", bit) for bit in reversed(bits_of(replicas))]
+
+
+def gather_rows(block):
+    parts = shard_parts()
+    spread = Spread(parts)
+    value = block.reshape((1,) * len(parts) + block.shape)
+    for part in parts:
+        value = grow(value, spread, part)
+    return value.reshape((-1, block.shape[1]))
+
+
+def gather_split(block, split_rows, order):
+    shard_bits = shard_parts()
+    replica_bits = replica_parts()
+    replicas, shards, r, _ = cells()
+    rows, columns = block.shape
+    parts = shard_bits + replica_bits
+    spread = Spread(parts)
+    if split_rows:
+        piece = lax.dynamic_slice_in_dim(block, r * (rows // replicas), rows // replicas, axis=0)
+    else:
+        piece = lax.dynamic_slice_in_dim(block, r * (columns // replicas), columns // replicas, axis=1)
+    value = piece.reshape((1,) * len(parts) + piece.shape)
+    for part in order(shard_bits, replica_bits):
+        value = grow(value, spread, part)
+    value = value.reshape((shards, replicas) + piece.shape)
+    if not split_rows:
+        value = jnp.concatenate([value[:, i] for i in range(replicas)], axis=-1)
+    return value.reshape(shards * rows, columns)
+
+
+def reduce_rows(grad):
+    parts = shard_parts()
+    spread = Spread(parts)
+    _, shards, _, _ = cells()
+    rows, columns = grad.shape
+    value = grad.reshape((2,) * len(parts) + (rows // shards, columns))
+    for part in reversed(parts):
+        value = halve(value, spread, part)
+    value = value.reshape(rows // shards, columns)
+    for part in replica_parts():
+        value = both(value, part)
+    return value
+
+
+def reduce_split(grad, split_rows, order):
+    shard_bits = shard_parts()
+    replica_bits = replica_parts()
+    replicas, shards, _, _ = cells()
+    rows, columns = grad.shape
+    own = rows // shards
+    parts = shard_bits + replica_bits
+    spread = Spread(parts)
+    if split_rows:
+        value = grad.reshape((2,) * len(parts) + (own // replicas, columns))
+    else:
+        width = columns // replicas
+        value = jnp.stack(
+            [grad[:, i * width : (i + 1) * width].reshape(shards, own, width) for i in range(replicas)],
+            axis=1,
+        ).reshape((2,) * len(parts) + (own, width))
+    done = []
+    for part in order(shard_bits, replica_bits):
+        value = halve(value, spread, part)
+        if part[0] == "r":
+            done.append(part)
+    value = low(value)
+    for part in reversed(done):
+        value = grow(value, spread, part)
+    value = value.reshape((replicas,) + value.shape[-2:])
+    if not split_rows:
+        value = jnp.concatenate([value[i] for i in range(replicas)], axis=-1)
+    return value.reshape(own, columns).astype(jnp.float32)
+
+
+def gather_zxy(shard_bits, replica_bits):
+    return shard_bits[:-1] + replica_bits + shard_bits[-1:]
+
+
+def gather_zyx(shard_bits, replica_bits):
+    return shard_bits[:-1] + replica_bits[::-1] + shard_bits[-1:]
+
+
+def gather_xyz(shard_bits, replica_bits):
+    return shard_bits[:1] + replica_bits + shard_bits[1:]
+
+
+def reduce_xyz(shard_bits, replica_bits):
+    return shard_bits[-1:] + replica_bits + shard_bits[:-1][::-1]
+
+
+def reduce_yxz(shard_bits, replica_bits):
+    return shard_bits[-1:] + replica_bits[::-1] + shard_bits[:-1][::-1]
+
+
+def reduce_zxy(shard_bits, replica_bits):
+    return shard_bits[-2:][::-1] + replica_bits + shard_bits[:-2][::-1]
 
 
 def layout(lengths_row, token_rows):
@@ -96,28 +273,21 @@
     offset, living, allowed = layout(seq_lengths[0], token_rows)
     cosine_table, sine_table = rotation(offset, HEAD_SIZE // 2)
     live_col = living[:, None]
-    gathered = (
-        lax.all_gather(w_query, "shard", axis=0, tiled=True),
-        lax.all_gather(key_weight, "shard", axis=0, tiled=True),
-        lax.all_gather(value_weight, "shard", axis=0, tiled=True),
-        lax.all_gather(w_out, "shard", axis=0, tiled=True),
-        lax.all_gather(w_gate, "shard", axis=0, tiled=True),
-        lax.all_gather(w_up, "shard", axis=0, tiled=True),
-        lax.all_gather(w_down, "shard", axis=0, tiled=True),
-        lax.all_gather(gain_attn, "shard", axis=0, tiled=True),
-        lax.all_gather(gain_ffn, "shard", axis=0, tiled=True),
-    )
-    (
-        full_query,
-        complete_key,
-        complete_value,
-        full_out,
-        full_gate,
-        full_up,
-        full_down,
-        full_gain_attn,
-        full_gain_ffn,
-    ) = gathered
+    first = gather_rows(
+        jnp.concatenate(
+            [w_query, key_weight, value_weight, gain_attn[:, None], gain_ffn[:, None]], axis=1
+        )
+    )
+    q_cols, kv_cols = w_query.shape[1], key_weight.shape[1]
+    full_query = first[:, :q_cols]
+    complete_key = first[:, q_cols : q_cols + kv_cols]
+    complete_value = first[:, q_cols + kv_cols : q_cols + 2 * kv_cols]
+    full_gain_attn = first[:, q_cols + 2 * kv_cols]
+    full_gain_ffn = first[:, q_cols + 2 * kv_cols + 1]
+    full_out = gather_rows(w_out)
+    full_gate = gather_split(w_gate, False, gather_zxy)
+    full_up = gather_split(w_up, False, gather_zyx)
+    full_down = gather_split(w_down, True, gather_xyz)
     masked = tokens.astype(jnp.float32) * live_col
     scale_one = rms_scale(masked)
     unit_one = masked * scale_one
@@ -163,49 +333,27 @@
     hidden = (silu_gate * up_proj).astype(jnp.bfloat16)
     ffn_out = matrix_product(hidden, full_down)
     output = (live_col * (middle + ffn_out)).astype(jnp.bfloat16)
-    again = (
-        lax.all_gather(w_query, "shard", axis=0, tiled=True),
-        lax.all_gather(key_weight, "shard", axis=0, tiled=True),
-        lax.all_gather(value_weight, "shard", axis=0, tiled=True),
-        lax.all_gather(w_out, "shard", axis=0, tiled=True),
-        lax.all_gather(w_gate, "shard", axis=0, tiled=True),
-        lax.all_gather(w_up, "shard", axis=0, tiled=True),
-        lax.all_gather(w_down, "shard", axis=0, tiled=True),
-        lax.all_gather(gain_attn, "shard", axis=0, tiled=True),
-        lax.all_gather(gain_ffn, "shard", axis=0, tiled=True),
-    )
-    (
-        back_query,
-        back_key,
-        back_value,
-        output_backward,
-        back_gate,
-        back_up,
-        back_down,
-        back_gain_attn,
-        back_gain_ffn,
-    ) = again
     grad_rows = cotangent.astype(jnp.float32) * live_col
     grad_ffn = grad_rows.astype(jnp.bfloat16)
     grad_down_w = rows_outer(hidden, grad_ffn)
-    grad_hidden = multiply_by_transpose(grad_ffn, back_down)
+    grad_hidden = multiply_by_transpose(grad_ffn, full_down)
     grad_gate_low = (
         grad_hidden * up_proj * sigmoid_gate * (1.0 + gate * (1.0 - sigmoid_gate))
     ).astype(jnp.bfloat16)
     grad_up_low = (grad_hidden * silu_gate).astype(jnp.bfloat16)
     grad_gate_w = rows_outer(normed_two, grad_gate_low)
     grad_up_w = rows_outer(normed_two, grad_up_low)
-    grad_normed_two = multiply_by_transpose(grad_gate_low, back_gate) + multiply_by_transpose(
-        grad_up_low, back_up
+    grad_normed_two = multiply_by_transpose(grad_gate_low, full_gate) + multiply_by_transpose(
+        grad_up_low, full_up
     )
     grad_gain_two = jnp.sum(grad_normed_two * unit_two, axis=0)
     grad_middle = grad_rows + norm_back(
-        grad_normed_two * back_gain_ffn.astype(jnp.float32), unit_two, scale_two
+        grad_normed_two * full_gain_ffn.astype(jnp.float32), unit_two, scale_two
     )
     attention_gradient_reduced = grad_middle.astype(jnp.bfloat16)
     grad_out_w = rows_outer(attn_low, attention_gradient_reduced)
     grad_attended = (
-        multiply_by_transpose(attention_gradient_reduced, output_backward)
+        multiply_by_transpose(attention_gradient_reduced, full_out)
         .astype(jnp.bfloat16)
         .reshape(token_rows, KEY_VALUE_HEADS, shard_group, HEAD_SIZE)
     )
@@ -247,43 +395,44 @@
     grad_key_w = rows_outer(normalized_input, grad_keys)
     grad_value_w = rows_outer(normalized_input, value_gradients_reduced)
     grad_normed = (
-        multiply_by_transpose(grad_queries, back_query)
-        + multiply_by_transpose(grad_keys, back_key)
-        + multiply_by_transpose(value_gradients_reduced, back_value)
+        multiply_by_transpose(grad_queries, full_query)
+        + multiply_by_transpose(grad_keys, complete_key)
+        + multiply_by_transpose(value_gradients_reduced, complete_value)
     )
     grad_gain_one = jnp.sum(grad_normed * unit_one, axis=0)
     grad_input = live_col * (
         grad_middle
-        + norm_back(grad_normed * back_gain_attn.astype(jnp.float32), unit_one, scale_one)
+        + norm_back(grad_normed * full_gain_attn.astype(jnp.float32), unit_one, scale_one)
     )
     grad_tokens = grad_input.astype(jnp.bfloat16)
-    owned = (
-        lax.psum_scatter(grad_query_w, "shard", scatter_dimension=0, tiled=True),
-        lax.psum_scatter(grad_key_w, "shard", scatter_dimension=0, tiled=True),
-        lax.psum_scatter(grad_value_w, "shard", scatter_dimension=0, tiled=True),
-        lax.psum_scatter(grad_out_w, "shard", scatter_dimension=0, tiled=True),
-        lax.psum_scatter(grad_gate_w, "shard", scatter_dimension=0, tiled=True),
-        lax.psum_scatter(grad_up_w, "shard", scatter_dimension=0, tiled=True),
-        lax.psum_scatter(grad_down_w, "shard", scatter_dimension=0, tiled=True),
-        lax.psum_scatter(grad_gain_one, "shard", scatter_dimension=0, tiled=True),
-        lax.psum_scatter(grad_gain_two, "shard", scatter_dimension=0, tiled=True),
-    )
-    summed = lax.psum(
-        (owned[0], owned[1], owned[2], owned[3], owned[4], owned[5], owned[6], owned[7], owned[8]),
-        "replica",
+    sum_down = reduce_split(grad_down_w, True, reduce_xyz)
+    sum_gate = reduce_split(grad_gate_w, False, reduce_yxz)
+    sum_up = reduce_split(grad_up_w, False, reduce_zxy)
+    sum_out = reduce_rows(grad_out_w)
+    last = reduce_rows(
+        jnp.concatenate(
+            [
+                grad_query_w,
+                grad_key_w,
+                grad_value_w,
+                grad_gain_one[:, None],
+                grad_gain_two[:, None],
+            ],
+            axis=1,
+        )
     )
     return (
         output,
         grad_tokens,
-        summed[0],
-        summed[1],
-        summed[2],
-        summed[3],
-        summed[4],
-        summed[5],
-        summed[6],
-        summed[7],
-        summed[8],
+        last[:, :q_cols],
+        last[:, q_cols : q_cols + kv_cols],
+        last[:, q_cols + kv_cols : q_cols + 2 * kv_cols],
+        sum_out,
+        sum_gate,
+        sum_up,
+        sum_down,
+        last[:, q_cols + 2 * kv_cols],
+        last[:, q_cols + 2 * kv_cols + 1],
     )
 
 

time: 994 us -> 667 us (0.67)
  waiting for transfers between devices: 596 us -> 194 us
  other arithmetic: 57.4 us -> 143 us
  blocking collectives: 76.5 us -> 0 us
  starting transfers between devices: 1.2 us -> 60.6 us
  local copies, waits for them, and re-layouts: 23.5 us -> 63.7 us
  matrix products: 215 us -> 193 us
  between operations: 16.5 us -> 2.98 us
    reduce_scatter x5 -> x0, waiting for transfers between devices: 413 us -> none  [the longest x1 110 us: body(): lax.psum_scatter(grad_down_w, 'shard', scatter_dimension=0, tiled=True)]
    ppermute x0 -> x52, waiting for transfers between devices: none -> 194 us  [swap(): return lax.ppermute(value, AXES, pairs)]
    all_gather x5 -> x0, waiting for transfers between devices: 86.9 us -> none  [the longest x1 46 us: body(): lax.all_gather(w_down, 'shard', axis=0, tiled=True)]
    psum x1 -> x0, waiting for transfers between devices: 79.7 us -> none  [body(): lax.psum((owned[0], owned[1], owned[2], owned[3], owned[4], owned[5], own...]
    ppermute x0 -> x52, starting transfers between devices: none -> 60.6 us  [swap(): return lax.ppermute(value, AXES, pairs)]
    all_gather x2 -> x0, blocking collectives: 33.4 us -> none  [the longest x1 17.9 us: body(): lax.all_gather(value_weight, 'shard', axis=0, tiled=True)]
    unnamed x2 -> x0, blocking collectives: 32.4 us -> none
    add x1 -> x21, other arithmetic: 0.91 us -> 28.6 us  [the longest x16 26.2 us: halve(): return keep.astype(jnp.float32) + other.astype(jnp.float32)]
  transfers between devices with their start and end apart: 12 -> 52, of which waited for: 9 -> 30; matrix products, arithmetic and copies ran while one was open for 16% -> 32% of each run, Pallas kernels for 0% -> 0%
where the time goes in v1:
time: 667 us; the launch traced here: 657 us
  waiting for transfers between devices  194 us (29%)
  matrix products  193 us (29%)
  other arithmetic  143 us (21%)
  local copies, waits for them, and re-layouts  63.7 us (10%)
  starting transfers between devices  60.6 us (9%)
    ppermute x52, waiting for transfers between devices, swap(): return lax.ppermute(value, AXES, pairs)  194 us
    ppermute x52, starting transfers between devices, swap(): return lax.ppermute(value, AXES, pairs)  60.6 us
    dot_general x7, matrix products, matrix_product(): return jnp.dot(left, right, preferred_element_type=jnp.float32)  33.6 us
    dot_general x7, matrix products, multiply_by_transpose(): jnp.einsum('rb,ab->ra', left, right, preferred_element_type=jnp.float32)  32.1 us
    convert_element_type x1, other arithmetic, body(): grad_scores = (probs_again * (grad_probs - row_delta)).astype(jnp.bfloat16)  30.3 us
    dot_general x7, matrix products, rows_outer(): jnp.einsum('ra,rb->ab', left, right, preferred_element_type=jnp.float32)  29.4 us
    dot_general x1, matrix products, body(): jnp.einsum('ikgd,jkd->kgij', grad_attended, v_low, preferred_element_type...  28.4 us
    add x16, other arithmetic, halve(): return keep.astype(jnp.float32) + other.astype(jnp.float32)  26.2 us
  transfers between devices with their start and end apart: 52, of which 30 were waited for; matrix products, arithmetic and copies ran while one was open for 32% of the time, Pallas kernels for 0%

profile of v1, /device:TPU:0, one launch (start us, length us, event | category | flops | bytes accessed | tf_op | source)
XLA Modules:
  0.0 657.3 jit_solution(16315690649305950557)
XLA Ops:
  23.8 10.7 %collective-permute-done.11 = bf16[1,1,1,1,1,120,640]{6,5,4,3,2,1,0:T(8,128)(2,1)S(1)} collective-permute-done((bf16[1,1,1,1,1,120,640]{6,5,4,3,2,1,0:T(8,128)(2,1)S(1)}, bf16[1,1,1,1,1,120,640]{6,5,4,3,2,1,0:T(8,128)(2,1)S(1)}, u32[]{:S(2)}, u32[]{:S(2)}) %collective-permute-start.11) | collective-permute-done | bytes 153632 | tf_op jit(solution)/shard_map/ppermute | solution.py:27
  47.9 6.6 %collective-permute-done = bf16[1,1,1,120,1602]{4,3,2,1,0:T(8,128)(2,1)} collective-permute-done((bf16[1,1,1,120,1602]{4,3,2,1,0:T(8,128)(2,1)S(1)}, bf16[1,1,1,120,1602]{4,3,2,1,0:T(8,128)(2,1)}, u32[]{:S(2)}, u32[]{:S(2)}) %collective-permute-start) | collective-permute-done | bytes 384512 | tf_op jit(solution)/shard_map/ppermute | solution.py:27
  56.3 4.7 collective-permute-done.12
  61.0 6.6 %collective-permute-done.7 = bf16[2,1,1,1,1,120,640]{6,5,4,3,2,1,0:T(8,128)(2,1)S(1)} collective-permute-done((bf16[2,1,1,1,1,120,640]{6,5,4,3,2,1,0:T(8,128)(2,1)S(1)}, bf16[2,1,1,1,1,120,640]{6,5,4,3,2,1,0:T(8,128)(2,1)S(1)}, u32[]{:S(2)}, u32[]{:S(2)}) %collective-permute-start.7) | collective-permute-done | bytes 307232 | tf_op jit(solution)/shard_map/ppermute | solution.py:27
  71.8 6.3 collective-permute-done.4
  78.4 5.2 collective-permute-done.8
  87.3 13.1 %collective-permute-done.18 = bf16[2,1,1,2,1,80,960]{6,5,4,3,2,1,0:T(8,128)(2,1)S(1)} collective-permute-done((bf16[2,1,1,2,1,80,960]{6,5,4,3,2,1,0:T(8,128)(2,1)S(1)}, bf16[2,1,1,2,1,80,960]{6,5,4,3,2,1,0:T(8,128)(2,1)S(1)}, u32[]{:S(2)}, u32[]{:S(2)}) %collective-permute-start.18) | collective-permute-done | bytes 614432 | tf_op jit(solution)/shard_map/ppermute | solution.py:27
  102.9 22.5 %collective-permute-done.9 = bf16[2,2,1,2,1,120,640]{6,5,4,3,2,1,0:T(8,128)(2,1)S(1)} collective-permute-done((bf16[2,2,1,2,1,120,640]{6,5,4,3,2,1,0:T(8,128)(2,1)S(1)}, bf16[2,2,1,2,1,120,640]{6,5,4,3,2,1,0:T(8,128)(2,1)S(1)}, u32[]{:S(2)}, u32[]{:S(2)}) %collective-permute-start.9) | collective-permute-done | bytes 1228832 | tf_op jit(solution)/shard_map/ppermute | solution.py:27
  144.3 14.4 %fusion.9 = (f32[5,3,768]{2,1,0:T(4,128)S(1)}, f32[5,768,768,3]{2,1,3,0:T(8,128)}) fusion(pred[768,768]{0,1:T(8,128)(4,1)S(1)} %fusion.16, bf16[768,5,3,32]{0,3,2,1:T(8,128)(2,1)S(1)} %bitcast.247, bf16[768,5,3,32]{0,3,2,1:T(8,128)(2,1)S(1)} %bitcast.245, bf16[768,5,32]{0,2,1:T(8,128)(2,1)S(1)} %get-tuple-element.108, ...), kind=kOutput, calls=%fused_computation.14 | convolution fusion | flops 1162924800 | bytes 37991424 | tf_op jit(solution)/shard_map/ikgd,jkd->kgij/dot_general | solution.py:312
  158.7 15.5 %fusion.3 = f32[5,3,768]{2,1,0:T(4,128)S(1)} fusion(f32[5,3,768]{2,1,0:T(4,128)S(1)} %get-tuple-element.151, f32[5,768,768,3]{2,1,3,0:T(8,128)} %get-tuple-element.152, pred[768,768]{0,1:T(8,128)(4,1)S(1)} %fusion.16), kind=kLoop, calls=%fused_computation.9 | loop fusion | flops 35377920 | bytes 36071424 | tf_op jit(solution)/shard_map/reduce_sum | solution.py:318
  174.2 17.7 %fusion.21 = bf16[5,64,3,768]{3,1,2,0:T(8,128)(2,1)} fusion(bf16[768,5,64,1]{0,2,3,1:T(8,128)(2,1)S(1)} %bitcast.281, f32[5,3,768]{2,1,0:T(4,128)S(1)} %fusion.3, f32[5,3,768]{2,1,0:T(4,128)S(1)} %get-tuple-element.151, f32[5,768,768,3]{2,1,3,0:T(8,128)} %get-tuple-element.152, pred[768,768]{0,1:T(8,128)(4,1)S(1)} %fusion.16), kind=kOutput, calls=%fused_computation.82 | convolution fusion | flops 1177436160 | bytes 38037504 | tf_op jit(solution)/shard_map/kgij,jkd->ikgd/dot_general | solution.py:321
  191.9 4.9 multiply_reduce_fusion.4
  214.8 6.9 %fusion.37 = f32[768,2560]{1,0:T(8,128)} fusion(bf16[768,960]{0,1:T(8,128)(2,1)S(1)} %multiply_convert_fusion.5, bf16[960,640]{1,0:T(8,128)(2,1)S(1)} %bitcast.266, bf16[960,640]{1,0:T(8,128)(2,1)S(1)} %bitcast.268, bf16[960,640]{1,0:T(8,128)(2,1)S(1)} %bitcast.270, bf16[960,640]{1,0:T(8,128)(2,1)S(1)} %bitcast.264), kind=kOutput, calls=%fused_computation.127 | convolution fusion | flops 3794534400 | bytes 14254080 | tf_op jit(solution)/shard_map/dot_general | solution.py:242
  221.8 8.4 %fusion.39 = f32[768,2560]{1,0:T(8,128)} fusion(bf16[768,960]{0,1:T(8,128)(2,1)} %copy-done.45, bf16[960,640]{1,0:T(8,128)(2,1)S(1)} %bitcast.274, bf16[960,640]{1,0:T(8,128)(2,1)S(1)} %bitcast.277, bf16[960,640]{1,0:T(8,128)(2,1)S(1)} %bitcast.279, bf16[960,640]{1,0:T(8,128)(2,1)S(1)} %bitcast.272), kind=kOutput, calls=%fused_computation.129 | convolution fusion | flops 3794534400 | bytes 14254080 | tf_op jit(solution)/shard_map/dot_general | solution.py:242
  230.2 13.3 %multiply_convert_fusion = (bf16[768,2560]{1,0:T(8,128)(2,1)}, bf16[768,2560]{1,0:T(8,128)(2,1)}, bf16[768,2560]{1,0:T(8,128)(2,1)}) fusion(f32[768,2560]{1,0:T(8,128)} %fusion.39, f32[768,2560]{1,0:T(8,128)} %fusion.37, bf16[2560,960]{1,0:T(8,128)(2,1)S(1)} %bitcast.243, bf16[768,960]{0,1:T(8,128)(2,1)S(1)} %copy-done.41, f32[768]{0:T(1024)S(1)} %get-tuple-element.162), kind=kOutput, calls=%fused_computation.17 | convolution fusion | flops 3806576640 | bytes 33917952 | tf_op jit(solution)/shard_map/rb,ab->ra/dot_general | solution.py:250
  243.5 6.9 %fusion.38 = f32[768,960]{0,1:T(8,128)S(1)} fusion(bf16[768,2560]{1,0:T(8,128)(2,1)} %get-tuple-element.53, bf16[960,640]{1,0:T(8,128)(2,1)S(1)} %bitcast.275, bf16[960,640]{1,0:T(8,128)(2,1)} %bitcast.276, bf16[960,640]{1,0:T(8,128)(2,1)} %bitcast.278, bf16[960,640]{1,0:T(8,128)(2,1)S(1)} %bitcast.273), kind=kOutput, calls=%fused_computation.128 | convolution fusion | flops 3794534400 | bytes 11796480 | tf_op jit(solution)/shard_map/rb,ab->ra/dot_general | solution.py:250
  250.4 6.5 fusion.72
  256.9 6.6 %fusion.73 = f32[960,2560]{1,0:T(8,128)} fusion(bf16[768,960]{0,1:T(8,128)(2,1)S(1)} %copy-done.46, bf16[768,2560]{1,0:T(8,128)(2,1)S(1)} %copy-done.71), kind=kOutput, calls=%fused_computation.271 | convolution fusion | flops 3774873600 | bytes 15237120 | tf_op jit(solution)/shard_map/ra,rb->ab/dot_general | solution.py:246
  263.6 4.4 multiply_reduce_fusion
  271.3 15.5 %fusion.33 = bf16[5,64,768]{2,1,0:T(8,128)(2,1)} fusion(bf16[768,5,3,64]{0,3,2,1:T(8,128)(2,1)S(1)} %bitcast.257, f32[5,3,768]{2,1,0:T(4,128)S(1)} %log_add_fusion, f32[5,768,768,3]{2,1,3,0:T(8,128)} %get-tuple-element.152, pred[768,768]{0,1:T(8,128)(4,1)S(1)} %fusion.16), kind=kOutput, calls=%fused_computation.109 | convolution fusion | flops 1168097280 | bytes 37991424 | tf_op jit(solution)/shard_map/kgij,ikgd->jkd/dot_general | solution.py:378
  286.8 28.4 %fusion = (f32[5,3,768]{2,1,0:T(4,128)S(1)}, f32[5,768,768,3]{2,1,3,0:T(8,128)}) fusion(f32[5,3,768]{2,1,0:T(4,128)S(1)} %log_add_fusion, f32[5,768,768,3]{2,1,3,0:T(8,128)} %get-tuple-element.152, pred[768,768]{0,1:T(8,128)(4,1)S(1)} %fusion.16, bf16[768,5,64,1]{0,2,3,1:T(8,128)(2,1)S(1)} %bitcast.282, bf16[768,5,3,64]{0,3,2,1:T(8,128)(2,1)S(1)} %bitcast.258), kind=kOutput, calls=%fused_computation.2 | convolution fusion | flops 1176687360 | bytes 73426944 | tf_op jit(solution)/shard_map/ikgd,jkd->kgij/dot_general | solution.py:366
  315.2 30.3 %fusion.2 = bf16[5,3,768,768]{2,3,1,0:T(8,128)(2,1)} fusion(f32[5,768,768,3]{2,1,3,0:T(8,128)} %get-tuple-element.157, f32[5,3,768]{2,1,0:T(4,128)S(1)} %get-tuple-element.156, f32[5,3,768]{2,1,0:T(4,128)S(1)} %log_add_fusion, f32[5,768,768,3]{2,1,3,0:T(8,128)} %get-tuple-element.152, pred[768,768]{0,1:T(8,128)(4,1)S(1)} %fusion.16), kind=kLoop, calls=%fused_computation.4 | loop fusion | flops 53084160 | bytes 89155584 | tf_op jit(solution)/shard_map/convert_element_type | solution.py:370
  345.6 12.5 %fusion.28 = f32[768,5,64]{0,2,1:T(8,128)} fusion(bf16[5,3,768,768]{2,3,1,0:T(8,128)(2,1)} %fusion.2, bf16[768,5,3,32]{0,3,2,1:T(8,128)(2,1)S(1)} %bitcast.248, bf16[768,5,3,32]{0,3,2,1:T(8,128)(2,1)S(1)} %bitcast.246), kind=kOutput, calls=%fused_computation.100 | convolution fusion | flops 1135656960 | bytes 20152320 | tf_op jit(solution)/shard_map/kgij,ikgd->jkd/dot_general | solution.py:375
  358.1 9.4 %convolution_multiply_fusion = f32[5,64,3,768]{3,1,2,0:T(8,128)S(1)} fusion(bf16[5,3,768,768]{2,3,1,0:T(8,128)(2,1)} %fusion.2, bf16[768,5,32]{0,2,1:T(8,128)(2,1)S(1)} %copy-done.62, bf16[768,5,32]{0,2,1:T(8,128)(2,1)S(1)} %copy-done.60), kind=kOutput, calls=%fused_computation.84 | convolution fusion | flops 1134182400 | bytes 21135360 | tf_op jit(solution)/shard_map/kgij,jkd->ikgd/dot_general | solution.py:372
  367.5 7.8 %multiply_convert_fusion.4 = bf16[768,960]{0,1:T(8,128)(2,1)} fusion(f32[768,960]{0,1:T(8,128)S(1)} %copy-done.14, bf16[768,2560]{1,0:T(8,128)(2,1)S(1)} %copy-done.73, bf16[2560,960]{1,0:T(8,128)(2,1)} %bitcast.244, f32[768]{0:T(1024)S(1)} %get-tuple-element.162), kind=kOutput, calls=%fused_computation.46 | convolution fusion | flops 3777085440 | bytes 13274112 | tf_op jit(solution)/shard_map/dot_general | solution.py:242
  383.3 4.5 fusion.63
  387.9 4.3 pad_maximum_fusion.1
  392.1 4.6 fusion.62
  401.2 4.5 fusion.65
  405.8 4.1 pad_maximum_fusion
  409.9 4.6 fusion.64
  435.6 8.4 %concatenate.181 = f32[2,2,2,120,1602]{4,3,2,1,0:T(8,128)} concatenate(f32[2,2,2,120,960]{4,3,2,1,0:T(8,128)} %fusion.69, f32[2,2,2,120,320]{4,3,2,1,0:T(8,128)} %fusion.70, f32[2,2,2,120,320]{4,3,2,1,0:T(8,128)} %fusion.71, f32[2,2,2,120,1]{4,3,2,1,0:T(8,128)S(1)} %concatenate.190, f32[2,2,2,120,1]{4,3,2,1,0:T(8,128)S(1)} %concatenate.191), dimensions={4} | concatenate | bytes 12303360 | tf_op jit(solution)/shard_map/concatenate | solution.py:413
  444.0 4.5 reduce-precision_convert_fusion.3
  448.8 4.5 fusion.29
  459.2 10.4 %collective-permute-done.27 = bf16[2,1,1,120,960]{4,3,2,1,0:T(8,128)(2,1)S(1)} collective-permute-done((bf16[2,1,1,120,960]{4,3,2,1,0:T(8,128)(2,1)S(1)}, bf16[2,1,1,120,960]{4,3,2,1,0:T(8,128)(2,1)S(1)}, u32[]{:S(2)}, u32[]{:S(2)}) %collective-permute-start.27) | collective-permute-done | bytes 460832 | tf_op jit(solution)/shard_map/ppermute | solution.py:27
  474.1 9.3 %collective-permute-done.28 = bf16[1,1,1,120,960]{4,3,2,1,0:T(8,128)(2,1)S(1)} collective-permute-done((bf16[1,1,1,120,960]{4,3,2,1,0:T(8,128)(2,1)S(1)}, bf16[1,1,1,120,960]{4,3,2,1,0:T(8,128)(2,1)S(1)}, u32[]{:S(2)}, u32[]{:S(2)}) %collective-permute-start.28) | collective-permute-done | bytes 230432 | tf_op jit(solution)/shard_map/ppermute | solution.py:27
  484.9 5.6 collective-permute-done.29
  497.7 5.1 collective-permute-done.22
  506.5 4.7 convert_add_fusion.1
  516.6 7.0 %collective-permute-done.23 = bf16[1,1,1,120,1602]{4,3,2,1,0:T(8,128)(2,1)S(1)} collective-permute-done((bf16[1,1,1,120,1602]{4,3,2,1,0:T(8,128)(2,1)S(1)}, bf16[1,1,1,120,1602]{4,3,2,1,0:T(8,128)(2,1)S(1)}, u32[]{:S(2)}, u32[]{:S(2)}) %collective-permute-start.23) | collective-permute-done | bytes 384512 | tf_op jit(solution)/shard_map/ppermute | solution.py:27
  535.7 6.5 convert_add_fusion
  546.0 21.0 %collective-permute-done.25 = bf16[120,1602]{1,0:T(8,128)(2,1)S(1)} collective-permute-done((bf16[120,1602]{1,0:T(8,128)(2,1)S(1)}, bf16[120,1602]{1,0:T(8,128)(2,1)S(1)}, u32[]{:S(2)}, u32[]{:S(2)}) %collective-permute-start.25) | collective-permute-done | bytes 384512 | tf_op jit(solution)/shard_map/ppermute | solution.py:27
  583.1 10.2 %collective-permute-done.40 = bf16[2,1,1,1,2,120,640]{6,5,4,3,2,1,0:T(8,128)(2,1)S(1)} collective-permute-done((bf16[2,1,1,1,2,120,640]{6,5,4,3,2,1,0:T(8,128)(2,1)S(1)}, bf16[2,1,1,1,2,120,640]{6,5,4,3,2,1,0:T(8,128)(2,1)S(1)}, u32[]{:S(2)}, u32[]{:S(2)}) %collective-permute-start.40) | collective-permute-done | bytes 614432 | tf_op jit(solution)/shard_map/ppermute | solution.py:27
  595.1 8.1 %collective-permute-done.33 = bf16[2,2,1,1,1,120,640]{6,5,4,3,2,1,0:T(8,128)(2,1)S(1)} collective-permute-done((bf16[2,2,1,1,1,120,640]{6,5,4,3,2,1,0:T(8,128)(2,1)S(1)}, bf16[2,2,1,1,1,120,640]{6,5,4,3,2,1,0:T(8,128)(2,1)S(1)}, u32[]{:S(2)}, u32[]{:S(2)}) %collective-permute-start.33) | collective-permute-done | bytes 614432 | tf_op jit(solution)/shard_map/ppermute | solution.py:27
  610.1 9.1 %collective-permute-done.34 = bf16[2,1,1,1,1,120,640]{6,5,4,3,2,1,0:T(8,128)(2,1)S(1)} collective-permute-done((bf16[2,1,1,1,1,120,640]{6,5,4,3,2,1,0:T(8,128)(2,1)S(1)}, bf16[2,1,1,1,1,120,640]{6,5,4,3,2,1,0:T(8,128)(2,1)S(1)}, u32[]{:S(2)}, u32[]{:S(2)}) %collective-permute-start.34) | collective-permute-done | bytes 307232 | tf_op jit(solution)/shard_map/ppermute | solution.py:27
  627.7 6.5 collective-permute-done.35
  643.8 4.5 collective-permute-done.44
  648.7 4.5 collective-permute-done.51
  (425 shorter events, 212.9 us)
Async XLA Ops:
  1.7 32.8 %collective-permute-start.11 = (bf16[1,1,1,1,1,120,640]{6,5,4,3,2,1,0:T(8,128)(2,1)S(1)}, bf16[1,1,1,1,1,120,640]{6,5,4,3,2,1,0:T(8,128)(2,1)S(1)}, u32[]{:S(2)}, u32[]{:S(2)}) collective-permute-start(bf16[1,1,1,1,1,120,640]{6,5,4,3,2,1,0:T(8,128)(2,1)S(1)} %dynamic-slice_bitcast_fusion.1), channel_id=1, source_target_pairs={{0,4},{1,5},{2,6},{3,7},{4,0},{5,1},{6,2},{7,3},{8,12},{9,13},{10,... | collective-permute-start | bytes 460808 | tf_op jit(solution)/shard_map/ppermute | solution.py:27
  6.7 31.3 %collective-permute-start.6 = (bf16[1,1,1,1,1,120,640]{6,5,4,3,2,1,0:T(8,128)(2,1)S(1)}, bf16[1,1,1,1,1,120,640]{6,5,4,3,2,1,0:T(8,128)(2,1)}, u32[]{:S(2)}, u32[]{:S(2)}) collective-permute-start(bf16[1,1,1,1,1,120,640]{6,5,4,3,2,1,0:T(8,128)(2,1)S(1)} %dynamic-slice_bitcast_fusion.2), channel_id=1, source_target_pairs={{0,4},{1,5},{2,6},{3,7},{4,0},{5,1},{6,2},{7,3},{8,12},{9,13},{10,... | collective-permute-start | bytes 460808 | tf_op jit(solution)/shard_map/ppermute | solution.py:27
  8.4 33.1 %collective-permute-start.16 = (bf16[1,1,1,1,1,80,960]{6,5,4,3,2,1,0:T(8,128)(2,1)}, bf16[1,1,1,1,1,80,960]{6,5,4,3,2,1,0:T(8,128)(2,1)}, u32[]{:S(2)}, u32[]{:S(2)}) collective-permute-start(bf16[1,1,1,1,1,80,960]{6,5,4,3,2,1,0:T(8,128)(2,1)} %dynamic-slice_bitcast_fusion), channel_id=1, source_target_pairs={{0,4},{1,5},{2,6},{3,7},{4,0},{5,1},{6,2},{7,3},{8,12},{9,13},{10,... | collective-permute-start | bytes 460808 | tf_op jit(solution)/shard_map/ppermute | solution.py:27
  11.3 35.5 %collective-permute-start.3 = (bf16[1,1,1,120,960]{4,3,2,1,0:T(8,128)(2,1)}, bf16[1,1,1,120,960]{4,3,2,1,0:T(8,128)(2,1)}, u32[]{:S(2)}, u32[]{:S(2)}) collective-permute-start(bf16[1,1,1,120,960]{4,3,2,1,0:T(8,128)(2,1)} %bitcast.285), channel_id=1, source_target_pairs={{0,4},{1,5},{2,6},{3,7},{4,0},{5,1},{6,2},{7,3},{8,12},{9,13},{10,... | collective-permute-start | bytes 691208 | tf_op jit(solution)/shard_map/ppermute | solution.py:27
  16.0 38.5 %collective-permute-start = (bf16[1,1,1,120,1602]{4,3,2,1,0:T(8,128)(2,1)S(1)}, bf16[1,1,1,120,1602]{4,3,2,1,0:T(8,128)(2,1)}, u32[]{:S(2)}, u32[]{:S(2)}) collective-permute-start(bf16[1,1,1,120,1602]{4,3,2,1,0:T(8,128)(2,1)S(1)} %bitcast.256), channel_id=1, source_target_pairs={{0,4},{1,5},{2,6},{3,7},{4,0},{5,1},{6,2},{7,3},{8,12},{9,13},{10,... | collective-permute-start | bytes 1153448 | tf_op jit(solution)/shard_map/ppermute | solution.py:27
  35.5 25.5 %collective-permute-start.12 = (bf16[2,1,1,1,1,120,640]{6,5,4,3,2,1,0:T(8,128)(2,1)S(1)}, bf16[2,1,1,1,1,120,640]{6,5,4,3,2,1,0:T(8,128)(2,1)S(1)}, u32[]{:S(2)}, u32[]{:S(2)}) collective-permute-start(bf16[2,1,1,1,1,120,640]{6,5,4,3,2,1,0:T(8,128)(2,1)S(1)} %pad_maximum_fusion.35), channel_id=1, source_target_pairs={{0,2},{1,3},{2,0},{3,1},{4,6},{5,7},{6,4},{7,5},{8,10},{9,11},{10,... | collective-permute-start | bytes 921608 | tf_op jit(solution)/shard_map/ppermute | solution.py:27
  39.1 28.5 %collective-permute-start.7 = (bf16[2,1,1,1,1,120,640]{6,5,4,3,2,1,0:T(8,128)(2,1)S(1)}, bf16[2,1,1,1,1,120,640]{6,5,4,3,2,1,0:T(8,128)(2,1)S(1)}, u32[]{:S(2)}, u32[]{:S(2)}) collective-permute-start(bf16[2,1,1,1,1,120,640]{6,5,4,3,2,1,0:T(8,128)(2,1)S(1)} %pad_maximum_fusion.34), channel_id=1, source_target_pairs={{0,2},{1,3},{2,0},{3,1},{4,6},{5,7},{6,4},{7,5},{8,10},{9,11},{10,... | collective-permute-start | bytes 921608 | tf_op jit(solution)/shard_map/ppermute | solution.py:27
  42.6 28.5 %collective-permute-start.17 = (bf16[2,1,1,1,1,80,960]{6,5,4,3,2,1,0:T(8,128)(2,1)S(1)}, bf16[2,1,1,1,1,80,960]{6,5,4,3,2,1,0:T(8,128)(2,1)S(1)}, u32[]{:S(2)}, u32[]{:S(2)}) collective-permute-start(bf16[2,1,1,1,1,80,960]{6,5,4,3,2,1,0:T(8,128)(2,1)S(1)} %pad_maximum_fusion.32), channel_id=1, source_target_pairs={{0,16},{1,17},{2,18},{3,19},{4,20},{5,21},{6,22},{7,23},{8,24},{9,... | collective-permute-start | bytes 921608 | tf_op jit(solution)/shard_map/ppermute | solution.py:27
  47.9 30.3 %collective-permute-start.4 = (bf16[2,1,1,120,960]{4,3,2,1,0:T(8,128)(2,1)S(1)}, bf16[2,1,1,120,960]{4,3,2,1,0:T(8,128)(2,1)S(1)}, u32[]{:S(2)}, u32[]{:S(2)}) collective-permute-start(bf16[2,1,1,120,960]{4,3,2,1,0:T(8,128)(2,1)S(1)} %pad_maximum_fusion.31), channel_id=1, source_target_pairs={{0,2},{1,3},{2,0},{3,1},{4,6},{5,7},{6,4},{7,5},{8,10},{9,11},{10,... | collective-permute-start | bytes 1382408 | tf_op jit(solution)/shard_map/ppermute | solution.py:27
  55.7 45.1 %collective-permute-start.1 = (bf16[2,1,1,120,1602]{4,3,2,1,0:T(8,128)(2,1)S(1)}, bf16[2,1,1,120,1602]{4,3,2,1,0:T(8,128)(2,1)S(1)}, u32[]{:S(2)}, u32[]{:S(2)}) collective-permute-start(bf16[2,1,1,120,1602]{4,3,2,1,0:T(8,128)(2,1)S(1)} %pad_maximum_fusion.24), channel_id=1, source_target_pairs={{0,2},{1,3},{2,0},{3,1},{4,6},{5,7},{6,4},{7,5},{8,10},{9,11},{10,... | collective-permute-start | bytes 2306888 | tf_op jit(solution)/shard_map/ppermute | solution.py:27
  67.8 15.7 %collective-permute-start.8 = (bf16[2,2,1,1,1,120,640]{6,5,4,3,2,1,0:T(8,128)(2,1)S(1)}, bf16[2,2,1,1,1,120,640]{6,5,4,3,2,1,0:T(8,128)(2,1)S(1)}, u32[]{:S(2)}, u32[]{:S(2)}) collective-permute-start(bf16[2,2,1,1,1,120,640]{6,5,4,3,2,1,0:T(8,128)(2,1)S(1)} %pad_maximum_fusion.27), channel_id=1, source_target_pairs={{0,16},{1,17},{2,18},{3,19},{4,20},{5,21},{6,22},{7,23},{8,24},{9,... | collective-permute-start | bytes 1843208 | tf_op jit(solution)/shard_map/ppermute | solution.py:27
  69.5 16.8 %collective-permute-start.13 = (bf16[2,2,1,1,1,120,640]{6,5,4,3,2,1,0:T(8,128)(2,1)S(1)}, bf16[2,2,1,1,1,120,640]{6,5,4,3,2,1,0:T(8,128)(2,1)S(1)}, u32[]{:S(2)}, u32[]{:S(2)}) collective-permute-start(bf16[2,2,1,1,1,120,640]{6,5,4,3,2,1,0:T(8,128)(2,1)S(1)} %pad_maximum_fusion.28), channel_id=1, source_target_pairs={{0,8},{1,9},{2,10},{3,11},{4,12},{5,13},{6,14},{7,15},{8,0},{9,1},... | collective-permute-start | bytes 1843208 | tf_op jit(solution)/shard_map/ppermute | solution.py:27
  71.2 29.2 %collective-permute-start.18 = (bf16[2,1,1,2,1,80,960]{6,5,4,3,2,1,0:T(8,128)(2,1)S(1)}, bf16[2,1,1,2,1,80,960]{6,5,4,3,2,1,0:T(8,128)(2,1)S(1)}, u32[]{:S(2)}, u32[]{:S(2)}) collective-permute-start(bf16[2,1,1,2,1,80,960]{6,5,4,3,2,1,0:T(8,128)(2,1)S(1)} %pad_maximum_fusion.25), channel_id=1, source_target_pairs={{0,8},{1,9},{2,10},{3,11},{4,12},{5,13},{6,14},{7,15},{8,0},{9,1},... | collective-permute-start | bytes 1843208 | tf_op jit(solution)/shard_map/ppermute | solution.py:27
  78.3 22.9 %collective-permute-start.5 = (bf16[2,2,1,120,960]{4,3,2,1,0:T(8,128)(2,1)S(1)}, bf16[2,2,1,120,960]{4,3,2,1,0:T(8,128)(2,1)S(1)}, u32[]{:S(2)}, u32[]{:S(2)}) collective-permute-start(bf16[2,2,1,120,960]{4,3,2,1,0:T(8,128)(2,1)S(1)} %pad_maximum_fusion.17), channel_id=1, source_target_pairs={{0,1},{1,0},{2,3},{3,2},{4,5},{5,4},{6,7},{7,6},{8,9},{9,8},{10,11... | collective-permute-start | bytes 2764808 | tf_op jit(solution)/shard_map/ppermute | solution.py:27
  83.9 41.5 %collective-permute-start.9 = (bf16[2,2,1,2,1,120,640]{6,5,4,3,2,1,0:T(8,128)(2,1)S(1)}, bf16[2,2,1,2,1,120,640]{6,5,4,3,2,1,0:T(8,128)(2,1)S(1)}, u32[]{:S(2)}, u32[]{:S(2)}) collective-permute-start(bf16[2,2,1,2,1,120,640]{6,5,4,3,2,1,0:T(8,128)(2,1)S(1)} %pad_maximum_fusion.15), channel_id=1, source_target_pairs={{0,8},{1,9},{2,10},{3,11},{4,12},{5,13},{6,14},{7,15},{8,0},{9,1},... | collective-permute-start | bytes 3686408 | tf_op jit(solution)/shard_map/ppermute | solution.py:27
  86.7 40.9 %collective-permute-start.14 = (bf16[2,2,1,1,2,120,640]{6,5,4,3,2,1,0:T(8,128)(2,1)S(1)}, bf16[2,2,1,1,2,120,640]{6,5,4,3,2,1,0:T(8,128)(2,1)S(1)}, u32[]{:S(2)}, u32[]{:S(2)}) collective-permute-start(bf16[2,2,1,1,2,120,640]{6,5,4,3,2,1,0:T(8,128)(2,1)S(1)} %pad_maximum_fusion.16), channel_id=1, source_target_pairs={{0,16},{1,17},{2,18},{3,19},{4,20},{5,21},{6,22},{7,23},{8,24},{9,... | collective-permute-start | bytes 3686408 | tf_op jit(solution)/shard_map/ppermute | solution.py:27
  100.7 29.6 %collective-permute-start.19 = (bf16[2,1,1,2,2,80,960]{6,5,4,3,2,1,0:T(8,128)(2,1)S(1)}, bf16[2,1,1,2,2,80,960]{6,5,4,3,2,1,0:T(8,128)(2,1)S(1)}, u32[]{:S(2)}, u32[]{:S(2)}) collective-permute-start(bf16[2,1,1,2,2,80,960]{6,5,4,3,2,1,0:T(8,128)(2,1)S(1)} %pad_maximum_fusion.14), channel_id=1, source_target_pairs={{0,2},{1,3},{2,0},{3,1},{4,6},{5,7},{6,4},{7,5},{8,10},{9,11},{10,... | collective-permute-start | bytes 3686408 | tf_op jit(solution)/shard_map/ppermute | solution.py:27
  101.1 31.4 %collective-permute-start.2 = (bf16[2,2,1,120,1602]{4,3,2,1,0:T(8,128)(2,1)S(1)}, bf16[2,2,1,120,1602]{4,3,2,1,0:T(8,128)(2,1)S(1)}, u32[]{:S(2)}, u32[]{:S(2)}) collective-permute-start(bf16[2,2,1,120,1602]{4,3,2,1,0:T(8,128)(2,1)S(1)} %pad_maximum_fusion.12), channel_id=1, source_target_pairs={{0,1},{1,0},{2,3},{3,2},{4,5},{5,4},{6,7},{7,6},{8,9},{9,8},{10,11... | collective-permute-start | bytes 4613768 | tf_op jit(solution)/shard_map/ppermute | solution.py:27
  127.6 72.8 %collective-permute-start.10 = (bf16[2,2,1,2,2,120,640]{6,5,4,3,2,1,0:T(8,128)(2,1)}, bf16[2,2,1,2,2,120,640]{6,5,4,3,2,1,0:T(8,128)(2,1)}, u32[]{:S(2)}, u32[]{:S(2)}) collective-permute-start(bf16[2,2,1,2,2,120,640]{6,5,4,3,2,1,0:T(8,128)(2,1)} %pad_maximum_fusion.9), channel_id=1, source_target_pairs={{0,1},{1,0},{2,3},{3,2},{4,5},{5,4},{6,7},{7,6},{8,9},{9,8},{10,11... | collective-permute-start | bytes 7372808 | tf_op jit(solution)/shard_map/ppermute | solution.py:27
  129.8 73.9 %collective-permute-start.15 = (bf16[2,2,1,2,2,120,640]{6,5,4,3,2,1,0:T(8,128)(2,1)}, bf16[2,2,1,2,2,120,640]{6,5,4,3,2,1,0:T(8,128)(2,1)}, u32[]{:S(2)}, u32[]{:S(2)}) collective-permute-start(bf16[2,2,1,2,2,120,640]{6,5,4,3,2,1,0:T(8,128)(2,1)} %pad_maximum_fusion.10), channel_id=1, source_target_pairs={{0,1},{1,0},{2,3},{3,2},{4,5},{5,4},{6,7},{7,6},{8,9},{9,8},{10,11... | collective-permute-start | bytes 7372808 | tf_op jit(solution)/shard_map/ppermute | solution.py:27
  132.5 77.9 %collective-permute-start.20 = (bf16[2,2,1,2,2,80,960]{6,5,4,3,2,1,0:T(8,128)(2,1)}, bf16[2,2,1,2,2,80,960]{6,5,4,3,2,1,0:T(8,128)(2,1)}, u32[]{:S(2)}, u32[]{:S(2)}) collective-permute-start(bf16[2,2,1,2,2,80,960]{6,5,4,3,2,1,0:T(8,128)(2,1)} %pad_maximum_fusion.8), channel_id=1, source_target_pairs={{0,1},{1,0},{2,3},{3,2},{4,5},{5,4},{6,7},{7,6},{8,9},{9,8},{10,11... | collective-permute-start | bytes 7372808 | tf_op jit(solution)/shard_map/ppermute | solution.py:27
  382.8 70.5 %collective-permute-start.26 = (bf16[2,2,1,120,960]{4,3,2,1,0:T(8,128)(2,1)}, bf16[2,2,1,120,960]{4,3,2,1,0:T(8,128)(2,1)}, u32[]{:S(2)}, u32[]{:S(2)}) collective-permute-start(bf16[2,2,1,120,960]{4,3,2,1,0:T(8,128)(2,1)} %reduce-precision_convert_fusion.7), channel_id=1, source_target_pairs={{0,1},{1,0},{2,3},{3,2},{4,5},{5,4},{6,7},{7,6},{8,9},{9,8},{10,11... | collective-permute-start | bytes 2764808 | tf_op jit(solution)/shard_map/ppermute | solution.py:27
  401.2 105.2 %collective-permute-start.38 = (bf16[2,2,1,2,2,120,640]{6,5,4,3,2,1,0:T(8,128)(2,1)}, bf16[2,2,1,2,2,120,640]{6,5,4,3,2,1,0:T(8,128)(2,1)}, u32[]{:S(2)}, u32[]{:S(2)}) collective-permute-start(bf16[2,2,1,2,2,120,640]{6,5,4,3,2,1,0:T(8,128)(2,1)} %reduce-precision_convert_fusion.1), channel_id=1, source_target_pairs={{0,1},{1,0},{2,3},{3,2},{4,5},{5,4},{6,7},{7,6},{8,9},{9,8},{10,11... | collective-permute-start | bytes 7372808 | tf_op jit(solution)/shard_map/ppermute | solution.py:27
  419.0 106.4 %collective-permute-start.31 = (bf16[2,2,1,2,2,120,640]{6,5,4,3,2,1,0:T(8,128)(2,1)}, bf16[2,2,1,2,2,120,640]{6,5,4,3,2,1,0:T(8,128)(2,1)}, u32[]{:S(2)}, u32[]{:S(2)}) collective-permute-start(bf16[2,2,1,2,2,120,640]{6,5,4,3,2,1,0:T(8,128)(2,1)} %reduce-precision_convert_fusion.2), channel_id=1, source_target_pairs={{0,1},{1,0},{2,3},{3,2},{4,5},{5,4},{6,7},{7,6},{8,9},{9,8},{10,11... | collective-permute-start | bytes 7372808 | tf_op jit(solution)/shard_map/ppermute | solution.py:27
  448.5 23.8 %collective-permute-start.21 = (bf16[2,2,1,120,1602]{4,3,2,1,0:T(8,128)(2,1)}, bf16[2,2,1,120,1602]{4,3,2,1,0:T(8,128)(2,1)}, u32[]{:S(2)}, u32[]{:S(2)}) collective-permute-start(bf16[2,2,1,120,1602]{4,3,2,1,0:T(8,128)(2,1)} %reduce-precision_convert_fusion.3), channel_id=1, source_target_pairs={{0,1},{1,0},{2,3},{3,2},{4,5},{5,4},{6,7},{7,6},{8,9},{9,8},{10,11... | collective-permute-start | bytes 4613768 | tf_op jit(solution)/shard_map/ppermute | solution.py:27
  456.1 13.4 %collective-permute-start.27 = (bf16[2,1,1,120,960]{4,3,2,1,0:T(8,128)(2,1)S(1)}, bf16[2,1,1,120,960]{4,3,2,1,0:T(8,128)(2,1)S(1)}, u32[]{:S(2)}, u32[]{:S(2)}) collective-permute-start(bf16[2,1,1,120,960]{4,3,2,1,0:T(8,128)(2,1)S(1)} %reduce-precision_convert_fusion.12), channel_id=1, source_target_pairs={{0,2},{1,3},{2,0},{3,1},{4,6},{5,7},{6,4},{7,5},{8,10},{9,11},{10,... | collective-permute-start | bytes 1382408 | tf_op jit(solution)/shard_map/ppermute | solution.py:27
  459.0 76.7 %collective-permute-start.45 = (bf16[2,2,1,2,2,80,960]{6,5,4,3,2,1,0:T(8,128)(2,1)}, bf16[2,2,1,2,2,80,960]{6,5,4,3,2,1,0:T(8,128)(2,1)}, u32[]{:S(2)}, u32[]{:S(2)}) collective-permute-start(bf16[2,2,1,2,2,80,960]{6,5,4,3,2,1,0:T(8,128)(2,1)} %reduce-precision_convert_fusion), channel_id=1, source_target_pairs={{0,1},{1,0},{2,3},{3,2},{4,5},{5,4},{6,7},{7,6},{8,9},{9,8},{10,11... | collective-permute-start | bytes 7372808 | tf_op jit(solution)/shard_map/ppermute | solution.py:27
  469.9 13.5 %collective-permute-start.28 = (bf16[1,1,1,120,960]{4,3,2,1,0:T(8,128)(2,1)S(1)}, bf16[1,1,1,120,960]{4,3,2,1,0:T(8,128)(2,1)S(1)}, u32[]{:S(2)}, u32[]{:S(2)}) collective-permute-start(bf16[1,1,1,120,960]{4,3,2,1,0:T(8,128)(2,1)S(1)} %reduce-precision_convert_fusion.21), channel_id=1, source_target_pairs={{0,4},{1,5},{2,6},{3,7},{4,0},{5,1},{6,2},{7,3},{8,12},{9,13},{10,... | collective-permute-start | bytes 691208 | tf_op jit(solution)/shard_map/ppermute | solution.py:27
  484.2 18.6 %collective-permute-start.22 = (bf16[2,1,1,120,1602]{4,3,2,1,0:T(8,128)(2,1)S(1)}, bf16[2,1,1,120,1602]{4,3,2,1,0:T(8,128)(2,1)S(1)}, u32[]{:S(2)}, u32[]{:S(2)}) collective-permute-start(bf16[2,1,1,120,1602]{4,3,2,1,0:T(8,128)(2,1)S(1)} %reduce-precision_convert_fusion.8), channel_id=1, source_target_pairs={{0,2},{1,3},{2,0},{3,1},{4,6},{5,7},{6,4},{7,5},{8,10},{9,11},{10,... | collective-permute-start | bytes 2306888 | tf_op jit(solution)/shard_map/ppermute | solution.py:27
  503.1 20.5 %collective-permute-start.23 = (bf16[1,1,1,120,1602]{4,3,2,1,0:T(8,128)(2,1)S(1)}, bf16[1,1,1,120,1602]{4,3,2,1,0:T(8,128)(2,1)S(1)}, u32[]{:S(2)}, u32[]{:S(2)}) collective-permute-start(bf16[1,1,1,120,1602]{4,3,2,1,0:T(8,128)(2,1)S(1)} %reduce-precision_convert_fusion.15), channel_id=1, source_target_pairs={{0,4},{1,5},{2,6},{3,7},{4,0},{5,1},{6,2},{7,3},{8,12},{9,13},{10,... | collective-permute-start | bytes 1153448 | tf_op jit(solution)/shard_map/ppermute | solution.py:27
  514.9 57.9 %collective-permute-start.39 = (bf16[2,1,1,2,2,120,640]{6,5,4,3,2,1,0:T(8,128)(2,1)}, bf16[2,1,1,2,2,120,640]{6,5,4,3,2,1,0:T(8,128)(2,1)}, u32[]{:S(2)}, u32[]{:S(2)}) collective-permute-start(bf16[2,1,1,2,2,120,640]{6,5,4,3,2,1,0:T(8,128)(2,1)} %reduce-precision_convert_fusion.5), channel_id=1, source_target_pairs={{0,2},{1,3},{2,0},{3,1},{4,6},{5,7},{6,4},{7,5},{8,10},{9,11},{10,... | collective-permute-start | bytes 3686408 | tf_op jit(solution)/shard_map/ppermute | solution.py:27
  523.7 10.2 %collective-permute-start.24 = (bf16[120,1602]{1,0:T(8,128)(2,1)S(1)}, bf16[120,1602]{1,0:T(8,128)(2,1)S(1)}, u32[]{:S(2)}, u32[]{:S(2)}) collective-permute-start(bf16[120,1602]{1,0:T(8,128)(2,1)S(1)} %fusion.48), channel_id=1, source_target_pairs={{0,16},{1,17},{2,18},{3,19},{4,20},{5,21},{6,22},{7,23},{8,24},{9,... | collective-permute-start | bytes 1153448 | tf_op jit(solution)/shard_map/ppermute | solution.py:27
  530.6 46.4 %collective-permute-start.32 = (bf16[2,2,1,2,1,120,640]{6,5,4,3,2,1,0:T(8,128)(2,1)}, bf16[2,2,1,2,1,120,640]{6,5,4,3,2,1,0:T(8,128)(2,1)}, u32[]{:S(2)}, u32[]{:S(2)}) collective-permute-start(bf16[2,2,1,2,1,120,640]{6,5,4,3,2,1,0:T(8,128)(2,1)} %reduce-precision_convert_fusion.6), channel_id=1, source_target_pairs={{0,8},{1,9},{2,10},{3,11},{4,12},{5,13},{6,14},{7,15},{8,0},{9,1},... | collective-permute-start | bytes 3686408 | tf_op jit(solution)/shard_map/ppermute | solution.py:27
  534.1 32.9 %collective-permute-start.25 = (bf16[120,1602]{1,0:T(8,128)(2,1)S(1)}, bf16[120,1602]{1,0:T(8,128)(2,1)S(1)}, u32[]{:S(2)}, u32[]{:S(2)}) collective-permute-start(bf16[120,1602]{1,0:T(8,128)(2,1)S(1)} %reduce-precision_convert_fusion.13), channel_id=1, source_target_pairs={{0,8},{1,9},{2,10},{3,11},{4,12},{5,13},{6,14},{7,15},{8,0},{9,1},... | collective-permute-start | bytes 1153448 | tf_op jit(solution)/shard_map/ppermute | solution.py:27
  544.5 35.9 %collective-permute-start.46 = (bf16[2,2,1,1,2,80,960]{6,5,4,3,2,1,0:T(8,128)(2,1)S(1)}, bf16[2,2,1,1,2,80,960]{6,5,4,3,2,1,0:T(8,128)(2,1)S(1)}, u32[]{:S(2)}, u32[]{:S(2)}) collective-permute-start(bf16[2,2,1,1,2,80,960]{6,5,4,3,2,1,0:T(8,128)(2,1)S(1)} %reduce-precision_convert_fusion.4), channel_id=1, source_target_pairs={{0,16},{1,17},{2,18},{3,19},{4,20},{5,21},{6,22},{7,23},{8,24},{9,... | collective-permute-start | bytes 3686408 | tf_op jit(solution)/shard_map/ppermute | solution.py:27
  576.5 16.9 %collective-permute-start.40 = (bf16[2,1,1,1,2,120,640]{6,5,4,3,2,1,0:T(8,128)(2,1)S(1)}, bf16[2,1,1,1,2,120,640]{6,5,4,3,2,1,0:T(8,128)(2,1)S(1)}, u32[]{:S(2)}, u32[]{:S(2)}) collective-permute-start(bf16[2,1,1,1,2,120,640]{6,5,4,3,2,1,0:T(8,128)(2,1)S(1)} %reduce-precision_convert_fusion.10), channel_id=1, source_target_pairs={{0,16},{1,17},{2,18},{3,19},{4,20},{5,21},{6,22},{7,23},{8,24},{9,... | collective-permute-start | bytes 1843208 | tf_op jit(solution)/shard_map/ppermute | solution.py:27
  579.1 24.2 %collective-permute-start.33 = (bf16[2,2,1,1,1,120,640]{6,5,4,3,2,1,0:T(8,128)(2,1)S(1)}, bf16[2,2,1,1,1,120,640]{6,5,4,3,2,1,0:T(8,128)(2,1)S(1)}, u32[]{:S(2)}, u32[]{:S(2)}) collective-permute-start(bf16[2,2,1,1,1,120,640]{6,5,4,3,2,1,0:T(8,128)(2,1)S(1)} %reduce-precision_convert_fusion.11), channel_id=1, source_target_pairs={{0,16},{1,17},{2,18},{3,19},{4,20},{5,21},{6,22},{7,23},{8,24},{9,... | collective-permute-start | bytes 1843208 | tf_op jit(solution)/shard_map/ppermute | solution.py:27
  581.5 24.6 %collective-permute-start.47 = (bf16[2,2,1,1,1,80,960]{6,5,4,3,2,1,0:T(8,128)(2,1)S(1)}, bf16[2,2,1,1,1,80,960]{6,5,4,3,2,1,0:T(8,128)(2,1)S(1)}, u32[]{:S(2)}, u32[]{:S(2)}) collective-permute-start(bf16[2,2,1,1,1,80,960]{6,5,4,3,2,1,0:T(8,128)(2,1)S(1)} %reduce-precision_convert_fusion.9), channel_id=1, source_target_pairs={{0,8},{1,9},{2,10},{3,11},{4,12},{5,13},{6,14},{7,15},{8,0},{9,1},... | collective-permute-start | bytes 1843208 | tf_op jit(solution)/shard_map/ppermute | solution.py:27
  593.6 13.0 %collective-permute-start.41 = (bf16[2,1,1,1,1,120,640]{6,5,4,3,2,1,0:T(8,128)(2,1)S(1)}, bf16[2,1,1,1,1,120,640]{6,5,4,3,2,1,0:T(8,128)(2,1)S(1)}, u32[]{:S(2)}, u32[]{:S(2)}) collective-permute-start(bf16[2,1,1,1,1,120,640]{6,5,4,3,2,1,0:T(8,128)(2,1)S(1)} %reduce-precision_convert_fusion.17), channel_id=1, source_target_pairs={{0,8},{1,9},{2,10},{3,11},{4,12},{5,13},{6,14},{7,15},{8,0},{9,1},... | collective-permute-start | bytes 921608 | tf_op jit(solution)/shard_map/ppermute | solution.py:27
  603.5 15.7 %collective-permute-start.34 = (bf16[2,1,1,1,1,120,640]{6,5,4,3,2,1,0:T(8,128)(2,1)S(1)}, bf16[2,1,1,1,1,120,640]{6,5,4,3,2,1,0:T(8,128)(2,1)S(1)}, u32[]{:S(2)}, u32[]{:S(2)}) collective-permute-start(bf16[2,1,1,1,1,120,640]{6,5,4,3,2,1,0:T(8,128)(2,1)S(1)} %reduce-precision_convert_fusion.18), channel_id=1, source_target_pairs={{0,2},{1,3},{2,0},{3,1},{4,6},{5,7},{6,4},{7,5},{8,10},{9,11},{10,... | collective-permute-start | bytes 921608 | tf_op jit(solution)/shard_map/ppermute | solution.py:27
  606.5 16.8 %collective-permute-start.48 = (bf16[2,1,1,1,1,80,960]{6,5,4,3,2,1,0:T(8,128)(2,1)S(1)}, bf16[2,1,1,1,1,80,960]{6,5,4,3,2,1,0:T(8,128)(2,1)S(1)}, u32[]{:S(2)}, u32[]{:S(2)}) collective-permute-start(bf16[2,1,1,1,1,80,960]{6,5,4,3,2,1,0:T(8,128)(2,1)S(1)} %reduce-precision_convert_fusion.16), channel_id=1, source_target_pairs={{0,2},{1,3},{2,0},{3,1},{4,6},{5,7},{6,4},{7,5},{8,10},{9,11},{10,... | collective-permute-start | bytes 921608 | tf_op jit(solution)/shard_map/ppermute | solution.py:27
  606.7 19.4 %collective-permute-start.42 = (bf16[1,1,1,1,1,120,640]{6,5,4,3,2,1,0:T(8,128)(2,1)S(1)}, bf16[1,1,1,1,1,120,640]{6,5,4,3,2,1,0:T(8,128)(2,1)S(1)}, u32[]{:S(2)}, u32[]{:S(2)}) collective-permute-start(bf16[1,1,1,1,1,120,640]{6,5,4,3,2,1,0:T(8,128)(2,1)S(1)} %reduce-precision_convert_fusion.25), channel_id=1, source_target_pairs={{0,4},{1,5},{2,6},{3,7},{4,0},{5,1},{6,2},{7,3},{8,12},{9,13},{10,... | collective-permute-start | bytes 460808 | tf_op jit(solution)/shard_map/ppermute | solution.py:27
  619.3 14.9 %collective-permute-start.35 = (bf16[1,1,1,1,1,120,640]{6,5,4,3,2,1,0:T(8,128)(2,1)S(1)}, bf16[1,1,1,1,1,120,640]{6,5,4,3,2,1,0:T(8,128)(2,1)S(1)}, u32[]{:S(2)}, u32[]{:S(2)}) collective-permute-start(bf16[1,1,1,1,1,120,640]{6,5,4,3,2,1,0:T(8,128)(2,1)S(1)} %reduce-precision_convert_fusion.27), channel_id=1, source_target_pairs={{0,4},{1,5},{2,6},{3,7},{4,0},{5,1},{6,2},{7,3},{8,12},{9,13},{10,... | collective-permute-start | bytes 460808 | tf_op jit(solution)/shard_map/ppermute | solution.py:27
  623.6 12.7 %collective-permute-start.49 = (bf16[1,1,1,1,1,80,960]{6,5,4,3,2,1,0:T(8,128)(2,1)S(1)}, bf16[1,1,1,1,1,80,960]{6,5,4,3,2,1,0:T(8,128)(2,1)S(1)}, u32[]{:S(2)}, u32[]{:S(2)}) collective-permute-start(bf16[1,1,1,1,1,80,960]{6,5,4,3,2,1,0:T(8,128)(2,1)S(1)} %reduce-precision_convert_fusion.23), channel_id=1, source_target_pairs={{0,4},{1,5},{2,6},{3,7},{4,0},{5,1},{6,2},{7,3},{8,12},{9,13},{10,... | collective-permute-start | bytes 460808 | tf_op jit(solution)/shard_map/ppermute | solution.py:27
  626.2 11.7 %collective-permute-start.43 = (bf16[1,1,1,1,1,120,640]{6,5,4,3,2,1,0:T(8,128)(2,1)S(1)}, bf16[1,1,1,1,1,120,640]{6,5,4,3,2,1,0:T(8,128)(2,1)S(1)}, u32[]{:S(2)}, u32[]{:S(2)}) collective-permute-start(bf16[1,1,1,1,1,120,640]{6,5,4,3,2,1,0:T(8,128)(2,1)S(1)} %reduce-precision_convert_fusion.24), channel_id=1, source_target_pairs={{0,8},{1,9},{2,10},{3,11},{4,12},{5,13},{6,14},{7,15},{8,0},{9,1},... | collective-permute-start | bytes 460808 | tf_op jit(solution)/shard_map/ppermute | solution.py:27
  638.0 10.3 %collective-permute-start.44 = (bf16[1,1,1,1,2,120,640]{6,5,4,3,2,1,0:T(8,128)(2,1)S(1)}, bf16[1,1,1,1,2,120,640]{6,5,4,3,2,1,0:T(8,128)(2,1)S(1)}, u32[]{:S(2)}, u32[]{:S(2)}) collective-permute-start(bf16[1,1,1,1,2,120,640]{6,5,4,3,2,1,0:T(8,128)(2,1)S(1)} %pad_maximum_fusion.37), channel_id=1, source_target_pairs={{0,16},{1,17},{2,18},{3,19},{4,20},{5,21},{6,22},{7,23},{8,24},{9,... | collective-permute-start | bytes 921608 | tf_op jit(solution)/shard_map/ppermute | solution.py:27
  640.2 8.3 %collective-permute-start.37 = (bf16[1,1,1,2,1,120,640]{6,5,4,3,2,1,0:T(8,128)(2,1)S(1)}, bf16[1,1,1,2,1,120,640]{6,5,4,3,2,1,0:T(8,128)(2,1)S(1)}, u32[]{:S(2)}, u32[]{:S(2)}) collective-permute-start(bf16[1,1,1,2,1,120,640]{6,5,4,3,2,1,0:T(8,128)(2,1)S(1)} %pad_maximum_fusion.36), channel_id=1, source_target_pairs={{0,8},{1,9},{2,10},{3,11},{4,12},{5,13},{6,14},{7,15},{8,0},{9,1},... | collective-permute-start | bytes 921608 | tf_op jit(solution)/shard_map/ppermute | solution.py:27
  643.6 9.5 %collective-permute-start.51 = (bf16[1,1,1,1,2,80,960]{6,5,4,3,2,1,0:T(8,128)(2,1)S(1)}, bf16[1,1,1,1,2,80,960]{6,5,4,3,2,1,0:T(8,128)(2,1)S(1)}, u32[]{:S(2)}, u32[]{:S(2)}) collective-permute-start(bf16[1,1,1,1,2,80,960]{6,5,4,3,2,1,0:T(8,128)(2,1)S(1)} %pad_maximum_fusion.33), channel_id=1, source_target_pairs={{0,16},{1,17},{2,18},{3,19},{4,20},{5,21},{6,22},{7,23},{8,24},{9,... | collective-permute-start | bytes 921608 | tf_op jit(solution)/shard_map/ppermute | solution.py:27
  (93 other events, 991.3 us)

commit v2 on v1

v2 whole, which is shorter than its diff:
```python
import jax
import jax.numpy as jnp
from jax import lax
from jax.experimental import pallas as pl
from jax.experimental.pallas import tpu as pltpu
from jax.sharding import PartitionSpec as P

QUERY_HEADS = 15
KEY_VALUE_HEADS = 5
HEAD_SIZE = 64


AXES = ("replica", "shard")


def cells():
    replicas = lax.axis_size("replica")
    shards = lax.axis_size("shard")
    return replicas, shards, lax.axis_index("replica"), lax.axis_index("shard")


def swap(value, kind, bit):
    replicas, shards, _, _ = cells()
    pairs = []
    for r in range(replicas):
        for s in range(shards):
            to = (r ^ bit) * shards + s if kind == "r" else r * shards + (s ^ bit)
            pairs.append((r * shards + s, to))
    return lax.ppermute(value, AXES, pairs)


def my_bit(kind, bit):
    _, _, r, s = cells()
    return ((r if kind == "r" else s) // bit) % 2


def bits_of(size):
    found = []
    bit = 1
    while bit < size:
        found.append(bit)
        bit *= 2
    return found


def low(value):
    return lax.reduce_precision(value.astype(jnp.float32), 8, 7).astype(jnp.bfloat16)


def grow(value, part, axis):
    other = swap(value, *part)
    upper = my_bit(*part) == 1
    first = jnp.where(upper, other, value)
    second = jnp.where(upper, value, other)
    return jnp.concatenate([first, second], axis=axis)


def add_low(mine, other):
    return low(mine.astype(jnp.float32) + other.astype(jnp.float32))


def halve(value, part, axis):
    upper = my_bit(*part) == 1
    lower_half = lax.slice_in_dim(value, 0, 1, axis=axis)
    upper_half = lax.slice_in_dim(value, 1, 2, axis=axis)
    keep = jnp.where(upper, upper_half, lower_half)
    send = jnp.where(upper, lower_half, upper_half)
    return add_low(keep, swap(send, *part))


def both(value, part):
    return add_low(value, swap(value, *part))


def shard_parts():
    _, shards, _, _ = cells()
    return [("s", bit) for bit in reversed(bits_of(shards))]


def replica_parts():
    replicas, _, _, _ = cells()
    return [("r", bit) for bit in reversed(bits_of(replicas))]


def gather_split(block, split_rows, order):
    shard_bits = shard_parts()
    replica_bits = replica_parts()
    replicas, shards, r, _ = cells()
    rows, columns = block.shape
    parts = shard_bits + replica_bits
    if split_rows:
        piece = lax.dynamic_slice_in_dim(block, r * (rows // replicas), rows // replicas, axis=0)
    else:
        piece = lax.dynamic_slice_in_dim(
            block, r * (columns // replicas), columns // replicas, axis=1
        )
    value = piece.reshape((1,) * len(parts) + piece.shape)
    for part in order(shard_bits, replica_bits):
        value = grow(value, part, parts.index(part))
        value = yield value
    value = value.reshape((shards, replicas) + piece.shape)
    if not split_rows:
        value = jnp.concatenate([value[:, i] for i in range(replicas)], axis=-1)
    yield value.reshape(shards * rows, columns)


def gather_rows(block):
    parts = shard_parts()
    value = block.reshape((1,) * len(parts) + block.shape)
    for part in parts:
        value = grow(value, part, parts.index(part))
        value = yield value
    yield value.reshape((-1, block.shape[1]))


def reduce_rows(grad):
    parts = shard_parts()
    _, shards, _, _ = cells()
    rows, columns = grad.shape
    value = grad.reshape((2,) * len(parts) + (rows // shards, columns))
    for part in reversed(parts):
        value = halve(value, part, parts.index(part))
        value = yield value
    value = value.reshape(rows // shards, columns)
    for part in replica_parts():
        value = both(value, part)
        value = yield value
    yield value.astype(jnp.float32)


def reduce_columns(left, right, half_bit, full_bits):
    parts = shard_parts()
    _, shards, _, _ = cells()
    rows, columns = left.shape
    shape = (2,) * len(parts) + (rows // shards, columns)
    core = parts[-1]
    axis = len(parts) - 1
    pair = (halve(left.reshape(shape), core, axis), halve(right.reshape(shape), core, axis))
    pair = yield pair
    upper = my_bit(*half_bit) == 1
    keep = jnp.where(upper, pair[1], pair[0])
    send = jnp.where(upper, pair[0], pair[1])
    value = add_low(keep, swap(send, *half_bit))
    value = yield value
    for part in reversed(parts[:-1]):
        value = halve(value, part, parts.index(part))
        value = yield value
    value = value.reshape(rows // shards, columns)
    for part in full_bits:
        value = both(value, part)
        value = yield value
    value = grow(value, half_bit, 1)
    value = yield value
    yield value.astype(jnp.float32)


class Flow:
    def __init__(self):
        self.running = []

    def add(self, steps):
        entry = [steps, None, False]
        self.running.append(entry)
        return entry

    def step(self, compute, inputs):
        moving = [e for e in self.running if not e[2]]
        held, inputs = lax.optimization_barrier(([e[1] for e in moving], inputs))
        for e, value in zip(moving, held):
            self.advance(e, value)
        result = list(compute(*inputs))
        moving = [e for e in moving if not e[2]]
        held, result[-1] = lax.optimization_barrier(([e[1] for e in moving], result[-1]))
        for e, value in zip(moving, held):
            e[1] = value
        return result

    def advance(self, entry, value):
        try:
            entry[1] = next(entry[0]) if value is None else entry[0].send(value)
        except StopIteration:
            entry[2] = True

    def finish(self, entry):
        while not entry[2]:
            self.advance(entry, entry[1])
        return entry[1]


def gather_zxy(shard_bits, replica_bits):
    return shard_bits[:-1] + replica_bits + shard_bits[-1:]


def gather_zyx(shard_bits, replica_bits):
    return shard_bits[:-1] + replica_bits[::-1] + shard_bits[-1:]


def gather_xyz(shard_bits, replica_bits):
    return shard_bits[:1] + replica_bits + shard_bits[1:]


def layout(lengths_row, token_rows):
    seq_ends = jnp.cumsum(lengths_row)
    positions = jnp.arange(token_rows, dtype=jnp.int32)
    passed = positions[:, None] >= seq_ends[None, :]
    segment = jnp.sum(passed.astype(jnp.int32), axis=1)
    seq_start = jnp.sum(jnp.where(passed, lengths_row[None, :], 0), axis=1)
    offset = (positions - seq_start).astype(jnp.float32)
    living = positions < seq_ends[-1]
    allowed = (
        (segment[:, None] == segment[None, :])
        & (positions[None, :] <= positions[:, None])
        & living[:, None]
    )
    allowed = allowed | (positions[:, None] == positions[None, :])
    return (offset, living.astype(jnp.float32), allowed)


def rotation(offset, half_dim):
    frequency = 10000.0 ** (-jnp.arange(half_dim, dtype=jnp.float32) / half_dim)
    angles = offset[:, None] * frequency[None, :]
    return (jnp.cos(angles)[:, None, :], jnp.sin(angles)[:, None, :])


def apply_rotary(values, cosine_table, sine_table):
    half_dim = values.shape[-1] // 2
    leading = values[..., :half_dim]
    trailing = values[..., half_dim:]
    return jnp.concatenate(
        [
            leading * cosine_table - trailing * sine_table,
            trailing * cosine_table + leading * sine_table,
        ],
        axis=-1,
    )


def reverse_rotary(gradient, cosine_table, sine_table):
    half_dim = gradient.shape[-1] // 2
    leading = gradient[..., :half_dim]
    trailing = gradient[..., half_dim:]
    return jnp.concatenate(
        [
            leading * cosine_table + trailing * sine_table,
            trailing * cosine_table - leading * sine_table,
        ],
        axis=-1,
    )


def rms_scale(values):
    return lax.rsqrt(jnp.mean(values * values, axis=-1, keepdims=True) + 1e-05)


def matrix_product(left, right):
    return jnp.dot(left, right, preferred_element_type=jnp.float32)


def rows_outer(left, right):
    return jnp.einsum("ra,rb->ab", left, right, preferred_element_type=jnp.float32)


def multiply_by_transpose(left, right):
    return jnp.einsum("rb,ab->ra", left, right, preferred_element_type=jnp.float32)


def norm_back(grad_unit, unit, scale):
    return scale * (grad_unit - unit * jnp.mean(grad_unit * unit, axis=-1, keepdims=True))


def row_block(rows):
    return 256 if rows % 256 == 0 else rows


def contract_last(left, right):
    return lax.dot_general(
        left, right, (((1,), (1,)), ((), ())), preferred_element_type=jnp.float32
    )


def contract_first(left, right):
    return lax.dot_general(
        left, right, (((0,), (0,)), ((), ())), preferred_element_type=jnp.float32
    )


def attend_kernel(q_ref, k_ref, v_ref, bias_ref, out_ref, lse_ref):
    group, rows = q_ref.shape[1], q_ref.shape[2]
    step = row_block(rows)
    for start in range(0, rows, step):
        reach = start + step
        keys = k_ref[0, :reach, :]
        values = v_ref[0, :reach, :]
        for head in range(group):
            scores = contract_last(q_ref[0, head, start:reach, :], keys) * 0.125
            scores = scores + bias_ref[start:reach, :reach]
            peak = jnp.max(scores, axis=-1, keepdims=True)
            raised = jnp.exp(scores - peak)
            total = jnp.sum(raised, axis=-1, keepdims=True)
            probs = (raised * (1.0 / total)).astype(jnp.bfloat16)
            out_ref[0, head, start:reach, :] = jnp.dot(
                probs, values, preferred_element_type=jnp.float32
            ).astype(jnp.bfloat16)
            lse_ref[0, start:reach, head : head + 1] = peak + jnp.log(total)


def unrope(value, cosine, sine):
    half = value.shape[-1] // 2
    swapped = jnp.concatenate([value[:, half:], value[:, :half]], axis=-1)
    return value * cosine + swapped * sine


def attend_back_kernel(
    q_ref, k_ref, v_ref, bias_ref, lse_ref, ga_ref, cos_ref, sin_ref, gq_ref, gk_ref, gv_ref, sk, sv
):
    group, rows = q_ref.shape[1], q_ref.shape[2]
    step = row_block(rows)
    sk[...] = jnp.zeros_like(sk)
    sv[...] = jnp.zeros_like(sv)
    for start in range(0, rows, step):
        reach = start + step
        keys = k_ref[0, :reach, :]
        values = v_ref[0, :reach, :]
        for head in range(group):
            queries = q_ref[0, head, start:reach, :]
            grads = ga_ref[0, head, start:reach, :]
            scores = contract_last(queries, keys) * 0.125 + bias_ref[start:reach, :reach]
            probs = jnp.exp(scores - lse_ref[0, start:reach, head : head + 1])
            grad_probs = contract_last(grads, values)
            delta = jnp.sum(probs * grad_probs, axis=-1, keepdims=True)
            grad_scores = (probs * (grad_probs - delta)).astype(jnp.bfloat16)
            grad_query = jnp.dot(grad_scores, keys, preferred_element_type=jnp.float32) * 0.125
            gq_ref[0, head, start:reach, :] = unrope(
                grad_query, cos_ref[start:reach, :], sin_ref[start:reach, :]
            ).astype(jnp.bfloat16)
            sk[:reach, :] += contract_first(grad_scores, queries)
            sv[:reach, :] += contract_first(probs.astype(jnp.bfloat16), grads)
    gk_ref[0] = unrope(sk[...] * 0.125, cos_ref[...], sin_ref[...]).astype(jnp.bfloat16)
    gv_ref[0] = sv[...].astype(jnp.bfloat16)


def head_spec(group, rows, size, base=0):
    return pl.BlockSpec((1, group, rows, size), lambda i: (i + base, 0, 0, 0))


def key_spec(rows, size, base=0):
    return pl.BlockSpec((1, rows, size), lambda i: (i + base, 0, 0))


def whole_spec(rows, columns):
    return pl.BlockSpec((rows, columns), lambda i: (0, 0))


def attend(query, key, value, bias, base, heads):
    _, group, rows, size = query.shape
    return pl.pallas_call(
        attend_kernel,
        grid=(heads,),
        in_specs=[
            head_spec(group, rows, size, base),
            key_spec(rows, size, base),
            key_spec(rows, size, base),
            whole_spec(rows, rows),
        ],
        out_specs=[head_spec(group, rows, size), key_spec(rows, group)],
        out_shape=[
            jax.ShapeDtypeStruct((heads, group, rows, size), jnp.bfloat16),
            jax.ShapeDtypeStruct((heads, rows, group), jnp.float32),
        ],
        compiler_params=pltpu.CompilerParams(vmem_limit_bytes=32 * 1024 * 1024),
        cost_estimate=pl.CostEstimate(
            flops=4 * heads * group * rows * rows * 256, bytes_accessed=12000000, transcendentals=0
        ),
    )(query, key, value, bias)


def attend_back(query, key, value, bias, lse, grad, cosine, sine, base, heads):
    _, group, rows, size = query.shape
    return pl.pallas_call(
        attend_back_kernel,
        grid=(heads,),
        in_specs=[
            head_spec(group, rows, size, base),
            key_spec(rows, size, base),
            key_spec(rows, size, base),
            whole_spec(rows, rows),
            key_spec(rows, group, base),
            head_spec(group, rows, size, base),
            whole_spec(rows, size),
            whole_spec(rows, size),
        ],
        out_specs=[head_spec(group, rows, size), key_spec(rows, size), key_spec(rows, size)],
        out_shape=[
            jax.ShapeDtypeStruct((heads, group, rows, size), jnp.bfloat16),
            jax.ShapeDtypeStruct((heads, rows, size), jnp.bfloat16),
            jax.ShapeDtypeStruct((heads, rows, size), jnp.bfloat16),
        ],
        scratch_shapes=[
            pltpu.VMEM((rows, size), jnp.float32),
            pltpu.VMEM((rows, size), jnp.float32),
        ],
        compiler_params=pltpu.CompilerParams(vmem_limit_bytes=32 * 1024 * 1024),
        cost_estimate=pl.CostEstimate(
            flops=10 * heads * group * rows * rows * 256, bytes_accessed=16000000, transcendentals=0
        ),
    )(query, key, value, bias, lse, grad, cosine, sine)


def body(
    tokens,
    cotangent,
    seq_lengths,
    w_query,
    key_weight,
    value_weight,
    w_out,
    w_gate,
    w_up,
    w_down,
    gain_attn,
    gain_ffn,
):
    token_rows = tokens.shape[0]
    shard_group = QUERY_HEADS // KEY_VALUE_HEADS
    offset, living, allowed = layout(seq_lengths[0], token_rows)
    cosine_table, sine_table = rotation(offset, HEAD_SIZE // 2)
    live_col = living[:, None]
    opening = Flow()
    first = opening.finish(opening.add(gather_rows(
        jnp.concatenate(
            [w_query, key_weight, value_weight, gain_attn[:, None], gain_ffn[:, None]], axis=1
        )
    )))
    q_cols, kv_cols = w_query.shape[1], key_weight.shape[1]
    full_query = first[:, :q_cols]
    complete_key = first[:, q_cols : q_cols + kv_cols]
    complete_value = first[:, q_cols + kv_cols : q_cols + 2 * kv_cols]
    full_gain_attn = first[:, q_cols + 2 * kv_cols]
    full_gain_ffn = first[:, q_cols + 2 * kv_cols + 1]
    full_gain_attn, w_out, w_gate, w_up, w_down = lax.optimization_barrier(
        (full_gain_attn, w_out, w_gate, w_up, w_down)
    )
    weights = Flow()
    coming_out = weights.add(gather_rows(w_out))
    coming_gate = weights.add(gather_split(w_gate, False, gather_zxy))
    coming_up = weights.add(gather_split(w_up, False, gather_zyx))
    coming_down = weights.add(gather_split(w_down, True, gather_xyz))
    masked = tokens.astype(jnp.float32) * live_col
    scale_one = rms_scale(masked)
    unit_one = masked * scale_one
    normalized_input = (unit_one * full_gain_attn.astype(jnp.float32)).astype(jnp.bfloat16)

    def project(normalized_input, full_query, complete_key, complete_value):
        query_rows = matrix_product(normalized_input, full_query).reshape(
            token_rows, QUERY_HEADS, HEAD_SIZE
        )
        unrotated_keys = matrix_product(normalized_input, complete_key).reshape(
            token_rows, KEY_VALUE_HEADS, HEAD_SIZE
        )
        projected_values = matrix_product(normalized_input, complete_value).reshape(
            token_rows, KEY_VALUE_HEADS, HEAD_SIZE
        )
        rotated_query = (
            apply_rotary(query_rows, cosine_table, sine_table)
            .astype(jnp.bfloat16)
            .reshape(token_rows, KEY_VALUE_HEADS, shard_group, HEAD_SIZE)
        )
        k_rot = apply_rotary(unrotated_keys, cosine_table, sine_table).astype(jnp.bfloat16)
        v_low = projected_values.astype(jnp.bfloat16)
        return (
            rotated_query.transpose(1, 2, 0, 3),
            k_rot.transpose(1, 0, 2),
            v_low.transpose(1, 0, 2),
        )

    heads_query, heads_key, heads_value = weights.step(
        lambda value: project(value, full_query, complete_key, complete_value), (normalized_input,)
    )
    bias = jnp.where(allowed, 0.0, -1e30).astype(jnp.float32)
    attended, log_total = [], []
    for base, heads in ((0, 1), (1, 2), (3, KEY_VALUE_HEADS - 3)):
        part, part_log = weights.step(
            lambda value: attend(heads_query, heads_key, value, bias, base, heads), (heads_value,)
        )
        attended.append(part)
        log_total.append(part_log)
    attended = jnp.concatenate(attended, axis=0)
    log_total = jnp.concatenate(log_total, axis=0)
    attn_low = attended.transpose(2, 0, 1, 3).reshape(token_rows, QUERY_HEADS * HEAD_SIZE)
    full_out = weights.finish(coming_out)
    full_gate = weights.finish(coming_gate)
    full_up = weights.finish(coming_up)
    full_down = weights.finish(coming_down)
    middle = masked + matrix_product(attn_low, full_out)
    scale_two = rms_scale(middle)
    unit_two = middle * scale_two
    normed_two = (unit_two * full_gain_ffn.astype(jnp.float32)).astype(jnp.bfloat16)
    gate = matrix_product(normed_two, full_gate)
    up_proj = matrix_product(normed_two, full_up)
    sigmoid_gate = jax.nn.sigmoid(gate)
    silu_gate = gate * sigmoid_gate
    hidden = (silu_gate * up_proj).astype(jnp.bfloat16)
    ffn_out = matrix_product(hidden, full_down)
    output = (live_col * (middle + ffn_out)).astype(jnp.bfloat16)
    grad_rows = cotangent.astype(jnp.float32) * live_col
    grad_ffn = grad_rows.astype(jnp.bfloat16)
    grads = Flow()
    replica_bits = replica_parts()
    sum_down = grads.add(reduce_rows(low(rows_outer(hidden, grad_ffn))))
    grad_hidden = multiply_by_transpose(grad_ffn, full_down)
    grad_gate_low = (
        grad_hidden * up_proj * sigmoid_gate * (1.0 + gate * (1.0 - sigmoid_gate))
    ).astype(jnp.bfloat16)
    grad_up_low = (grad_hidden * silu_gate).astype(jnp.bfloat16)
    half = grad_gate_low.shape[1] // 2
    sum_gate = grads.add(
        reduce_columns(
            low(rows_outer(normed_two, grad_gate_low[:, :half])),
            low(rows_outer(normed_two, grad_gate_low[:, half:])),
            replica_bits[0],
            replica_bits[1:],
        )
    )
    sum_up = grads.add(
        reduce_columns(
            low(rows_outer(normed_two, grad_up_low[:, :half])),
            low(rows_outer(normed_two, grad_up_low[:, half:])),
            replica_bits[-1],
            replica_bits[:-1],
        )
    )
    (grad_normed_two,) = grads.step(
        lambda up_low: (
            multiply_by_transpose(grad_gate_low, full_gate)
            + multiply_by_transpose(up_low, full_up),
        ),
        (grad_up_low,),
    )
    grad_gain_two = jnp.sum(grad_normed_two * unit_two, axis=0)
    grad_middle = grad_rows + norm_back(
        grad_normed_two * full_gain_ffn.astype(jnp.float32), unit_two, scale_two
    )
    attention_gradient_reduced = grad_middle.astype(jnp.bfloat16)
    sum_out = grads.add(reduce_rows(low(rows_outer(attn_low, attention_gradient_reduced))))
    grad_attended = (
        multiply_by_transpose(attention_gradient_reduced, full_out)
        .astype(jnp.bfloat16)
        .reshape(token_rows, KEY_VALUE_HEADS, shard_group, HEAD_SIZE)
    )
    both_cosine = jnp.concatenate([cosine_table[:, 0], cosine_table[:, 0]], axis=-1)
    both_sine = jnp.concatenate([sine_table[:, 0], -sine_table[:, 0]], axis=-1)
    inputs = (
        heads_query,
        heads_key,
        heads_value,
        bias,
        log_total,
        grad_attended.transpose(1, 2, 0, 3),
        both_cosine,
    )
    pieces = []
    for base, heads in ((0, 2), (2, 1), (3, 1), (4, KEY_VALUE_HEADS - 4)):
        pieces.append(grads.step(lambda sine: attend_back(*inputs, sine, base, heads), (both_sine,)))
    heads_gq, heads_gk, heads_gv = [jnp.concatenate(p, axis=0) for p in zip(*pieces)]
    grad_queries = heads_gq.transpose(2, 0, 1, 3).reshape(token_rows, QUERY_HEADS * HEAD_SIZE)
    grad_keys = heads_gk.transpose(1, 0, 2).reshape(token_rows, KEY_VALUE_HEADS * HEAD_SIZE)
    value_gradients_reduced = heads_gv.transpose(1, 0, 2).reshape(
        token_rows, KEY_VALUE_HEADS * HEAD_SIZE
    )
    grad_query_w = rows_outer(normalized_input, grad_queries)
    grad_key_w = rows_outer(normalized_input, grad_keys)
    grad_value_w = rows_outer(normalized_input, value_gradients_reduced)
    grad_normed = (
        multiply_by_transpose(grad_queries, full_query)
        + multiply_by_transpose(grad_keys, complete_key)
        + multiply_by_transpose(value_gradients_reduced, complete_value)
    )
    grad_gain_one = jnp.sum(grad_normed * unit_one, axis=0)
    grad_input = live_col * (
        grad_middle
        + norm_back(grad_normed * full_gain_attn.astype(jnp.float32), unit_one, scale_one)
    )
    grad_tokens = grad_input.astype(jnp.bfloat16)
    last = grads.add(reduce_rows(low(
        jnp.concatenate(
            [
                grad_query_w,
                grad_key_w,
                grad_value_w,
                grad_gain_one[:, None],
                grad_gain_two[:, None],
            ],
            axis=1,
        )
    )))
    last, sum_out, sum_gate, sum_up, sum_down = [
        grads.finish(e) for e in (last, sum_out, sum_gate, sum_up, sum_down)
    ]
    return (
        output,
        grad_tokens,
        last[:, :q_cols],
        last[:, q_cols : q_cols + kv_cols],
        last[:, q_cols + kv_cols : q_cols + 2 * kv_cols],
        sum_out,
        sum_gate,
        sum_up,
        sum_down,
        last[:, q_cols + 2 * kv_cols],
        last[:, q_cols + 2 * kv_cols + 1],
    )


def solution(mesh):
    return jax.shard_map(
        body,
        mesh=mesh,
        in_specs=(
            P(("replica", "shard"), None),
            P(("replica", "shard"), None),
            P(("replica", "shard"), None),
            P("shard", None),
            P("shard", None),
            P("shard", None),
            P("shard", None),
            P("shard", None),
            P("shard", None),
            P("shard", None),
            P("shard"),
            P("shard"),
        ),
        out_specs=(
            P(("replica", "shard"), None),
            P(("replica", "shard"), None),
            P("shard", None),
            P("shard", None),
            P("shard", None),
            P("shard", None),
            P("shard", None),
            P("shard", None),
            P("shard", None),
            P("shard"),
            P("shard"),
        ),
        check_vma=False,
    )
```

time: 667 us -> 632 us (0.948)
  matrix products: 193 us -> 110 us
  Pallas kernels: 0 us -> 50.3 us
  local copies, waits for them, and re-layouts: 63.7 us -> 110 us
  other arithmetic: 143 us -> 107 us
  starting transfers between devices: 60.6 us -> 52.2 us
    dot_general x6 -> x0, matrix products: 97.8 us -> none  [the longest x1 28.4 us: body(): jnp.einsum('ikgd,jkd->kgij', grad_attended, v_low, preferred_element_type...]
    pallas_call x0 -> x7, Pallas kernels: none -> 50.3 us  [the longest x4 30.3 us: attend_back(): pl.pallas_call(attend_back_kernel, grid=(heads,), in_specs=[head_spec(gro...]
    convert_element_type x6, other arithmetic: 34 us -> 4.49 us  [the longest x2 2.3 us: reduce_columns(): yield value.astype(jnp.float32)]
    add x21 -> x0, other arithmetic: 27.7 us -> none  [the longest x16 26.2 us: halve(): return keep.astype(jnp.float32) + other.astype(jnp.float32)]
    unnamed x184 -> x239, local copies, waits for them, and re-layouts: 24.3 us -> 44.4 us
    transpose x0 -> x4, local copies, waits for them, and re-layouts: none -> 18.5 us  [the longest x1 12.6 us: body(): attended.transpose(2, 0, 1, 3).reshape(token_rows, QUERY_HEADS * HEAD_SIZE)]
    select_n x0 -> x20, other arithmetic: none -> 15.4 us  [the longest x17 11.2 us: halve(): send = jnp.where(upper, lower_half, upper_half)]
    reduce_sum x1, other arithmetic: 15.5 us -> 0.91 us  [body(): grad_gain_two = jnp.sum(grad_normed_two * unit_two, axis=0)]
  transfers between devices with their start and end apart: 52 -> 50, of which waited for: 30 -> 19; matrix products, arithmetic and copies ran while one was open for 32% -> 25% of each run, Pallas kernels for 0% -> 7%
where the time goes in v2:
time: 632 us; the launch traced here: 621 us
  waiting for transfers between devices  189 us (30%)
  local copies, waits for them, and re-layouts  110 us (17%)
  matrix products  110 us (17%)
  other arithmetic  107 us (17%)
  starting transfers between devices  52.2 us (8%)
  Pallas kernels  50.3 us (8%)
    ppermute x50, waiting for transfers between devices, swap(): return lax.ppermute(value, AXES, pairs)  189 us
    ppermute x50, starting transfers between devices, swap(): return lax.ppermute(value, AXES, pairs)  52.2 us
    unnamed x239, local copies, waits for them, and re-layouts  44.4 us
    dot_general x7, matrix products, multiply_by_transpose(): jnp.einsum('rb,ab->ra', left, right, preferred_element_type=jnp.float32)  43 us
    dot_general x9, matrix products, rows_outer(): jnp.einsum('ra,rb->ab', left, right, preferred_element_type=jnp.float32)  34.2 us
    convert_element_type x25, other arithmetic, low(): lax.reduce_precision(value.astype(jnp.float32), 8, 7).astype(jnp.bfloat16)  33 us
    dot_general x7, matrix products, matrix_product(): return jnp.dot(left, right, preferred_element_type=jnp.float32)  33 us
    pallas_call x4, Pallas kernels, attend_back(): pl.pallas_call(attend_back_kernel, grid=(heads,), in_specs=[head_spec(gro...  30.3 us
  transfers between devices with their start and end apart: 50, of which 19 were waited for; matrix products, arithmetic and copies ran while one was open for 25% of the time, Pallas kernels for 7%

profile of v2, /device:TPU:0, one launch (start us, length us, event | category | flops | bytes accessed | tf_op | source)
XLA Modules:
  0.0 621.5 jit_solution(10733689158616915459)
XLA Ops:
  5.3 4.1 collective-permute-start
  9.4 17.8 %collective-permute-done = bf16[1,1,1,120,1602]{4,3,2,1,0:T(8,128)(2,1)S(1)} collective-permute-done((bf16[1,1,1,120,1602]{4,3,2,1,0:T(8,128)(2,1)S(1)}, bf16[1,1,1,120,1602]{4,3,2,1,0:T(8,128)(2,1)S(1)}, u32[]{:S(2)}, u32[]{:S(2)}) %collective-permute-start) | collective-permute-done | bytes 384512 | tf_op jit(solution)/shard_map/ppermute | solution.py:29
  29.0 17.5 %collective-permute-done.1 = bf16[2,1,1,120,1602]{4,3,2,1,0:T(8,128)(2,1)S(1)} collective-permute-done((bf16[2,1,1,120,1602]{4,3,2,1,0:T(8,128)(2,1)S(1)}, bf16[2,1,1,120,1602]{4,3,2,1,0:T(8,128)(2,1)S(1)}, u32[]{:S(2)}, u32[]{:S(2)}) %collective-permute-start.1) | collective-permute-done | bytes 768992 | tf_op jit(solution)/shard_map/ppermute | solution.py:29
  76.8 3.7 fusion.41
  80.5 4.9 copy.125
  85.4 4.8 copy.124
  93.5 3.8 subtract_convert_fusion
  109.5 4.0 shard_map.203
  113.8 6.5 %collective-permute-done.9 = bf16[2,1,1,1,1,120,640]{6,5,4,3,2,1,0:T(8,128)(2,1)S(1)} collective-permute-done((bf16[2,1,1,1,1,120,640]{6,5,4,3,2,1,0:T(8,128)(2,1)S(1)}, bf16[2,1,1,1,1,120,640]{6,5,4,3,2,1,0:T(8,128)(2,1)S(1)}, u32[]{:S(2)}, u32[]{:S(2)}) %collective-permute-start.9) | collective-permute-done | bytes 307232 | tf_op jit(solution)/shard_map/ppermute | solution.py:29
  123.1 6.4 %collective-permute-done.7 = bf16[2,1,1,120,960]{4,3,2,1,0:T(8,128)(2,1)S(1)} collective-permute-done((bf16[2,1,1,120,960]{4,3,2,1,0:T(8,128)(2,1)S(1)}, bf16[2,1,1,120,960]{4,3,2,1,0:T(8,128)(2,1)S(1)}, u32[]{:S(2)}, u32[]{:S(2)}) %collective-permute-start.7) | collective-permute-done | bytes 460832 | tf_op jit(solution)/shard_map/ppermute | solution.py:29
  138.2 8.0 %shard_map.204 = (bf16[2,3,768,64]{3,2,1,0:T(8,128)(2,1)S(1)}, f32[2,768,3]{2,1,0:T(8,128)S(1)}) custom-call(bf16[5,3,768,64]{3,2,1,0:T(8,128)(2,1)S(1)} %maximum_bitcast_fusion.q_ref, bf16[5,768,64]{2,1,0:T(8,128)(2,1)S(1)} %copy-done.7, bf16[5,768,64]{2,1,0:T(8,128)(2,1)S(1)} %bitcast.122, f32[768,768]{1,0:T(8,128)S(1)} %copy-done.1), custom_call_target="tpu_custom_call" | custom-call | flops 3623878656 | bytes 12000000 | tf_op jit(solution)/shard_map/pallas_call | solution.py:356
  149.4 11.2 %collective-permute-done.14 = bf16[2,1,1,2,1,80,960]{6,5,4,3,2,1,0:T(8,128)(2,1)S(1)} collective-permute-done((bf16[2,1,1,2,1,80,960]{6,5,4,3,2,1,0:T(8,128)(2,1)}, bf16[2,1,1,2,1,80,960]{6,5,4,3,2,1,0:T(8,128)(2,1)S(1)}, u32[]{:S(2)}, u32[]{:S(2)}) %collective-permute-start.14) | collective-permute-done | bytes 614432 | tf_op jit(solution)/shard_map/ppermute | solution.py:29
  166.2 8.0 %shard_map.205 = (bf16[2,3,768,64]{3,2,1,0:T(8,128)(2,1)S(1)}, f32[2,768,3]{2,1,0:T(8,128)S(1)}) custom-call(bf16[5,3,768,64]{3,2,1,0:T(8,128)(2,1)S(1)} %maximum_bitcast_fusion.q_ref, bf16[5,768,64]{2,1,0:T(8,128)(2,1)S(1)} %copy-done.7, bf16[5,768,64]{2,1,0:T(8,128)(2,1)S(1)} %bitcast.123, f32[768,768]{1,0:T(8,128)S(1)} %copy-done.1), custom_call_target="tpu_custom_call" | custom-call | flops 3623878656 | bytes 12000000 | tf_op jit(solution)/shard_map/pallas_call | solution.py:356
  174.2 14.7 %collective-permute-done.15 = bf16[2,2,1,2,1,120,640]{6,5,4,3,2,1,0:T(8,128)(2,1)S(1)} collective-permute-done((bf16[2,2,1,2,1,120,640]{6,5,4,3,2,1,0:T(8,128)(2,1)S(1)}, bf16[2,2,1,2,1,120,640]{6,5,4,3,2,1,0:T(8,128)(2,1)S(1)}, u32[]{:S(2)}, u32[]{:S(2)}) %collective-permute-start.15) | collective-permute-done | bytes 1228832 | tf_op jit(solution)/shard_map/ppermute | solution.py:29
  201.6 3.9 maximum_bitcast_fusion.1
  205.5 12.6 %copy.98 = bf16[768,5,3,64]{0,3,2,1:T(8,128)(2,1)} copy(bf16[768,5,3,64]{3,0,2,1:T(8,128)(2,1)} %maximum_bitcast_fusion.1) | data formatting | bytes 2949120 | tf_op jit(solution)/shard_map/transpose | solution.py:489
  221.4 4.4 multiply_reduce_fusion.4
  241.2 7.0 %fusion.19 = f32[768,2560]{1,0:T(8,128)} fusion(bf16[768,960]{0,1:T(8,128)(2,1)S(1)} %multiply_convert_fusion.5, bf16[960,640]{1,0:T(8,128)(2,1)S(1)} %bitcast.178, bf16[960,640]{1,0:T(8,128)(2,1)S(1)} %bitcast.180, bf16[960,640]{1,0:T(8,128)(2,1)S(1)} %bitcast.182, bf16[960,640]{1,0:T(8,128)(2,1)S(1)} %bitcast.176), kind=kOutput, calls=%fused_computation.115 | convolution fusion | flops 3794534400 | bytes 14254080 | tf_op jit(solution)/shard_map/dot_general | solution.py:256
  248.2 8.4 %fusion.21 = f32[768,2560]{1,0:T(8,128)} fusion(bf16[768,960]{0,1:T(8,128)(2,1)} %copy-done.80, bf16[960,640]{1,0:T(8,128)(2,1)S(1)} %bitcast.186, bf16[960,640]{1,0:T(8,128)(2,1)S(1)} %bitcast.188, bf16[960,640]{1,0:T(8,128)(2,1)S(1)} %bitcast.190, bf16[960,640]{1,0:T(8,128)(2,1)S(1)} %bitcast.184), kind=kOutput, calls=%fused_computation.117 | convolution fusion | flops 3794534400 | bytes 14254080 | tf_op jit(solution)/shard_map/dot_general | solution.py:256
  256.6 13.6 %multiply_convert_fusion = (bf16[768,2560]{1,0:T(8,128)(2,1)}, bf16[768,2560]{1,0:T(8,128)(2,1)}, bf16[768,2560]{1,0:T(8,128)(2,1)}) fusion(f32[768,2560]{1,0:T(8,128)} %fusion.21, f32[768,2560]{1,0:T(8,128)} %fusion.19, bf16[2560,960]{1,0:T(8,128)(2,1)S(1)} %bitcast.155, bf16[768,960]{0,1:T(8,128)(2,1)S(1)} %copy-done.75, f32[768]{0:T(1024)S(1)} %get-tuple-element.341), kind=kOutput, calls=%fused_computation.1 | convolution fusion | flops 3806576640 | bytes 33917952 | tf_op jit(solution)/shard_map/rb,ab->ra/dot_general | solution.py:264
  270.2 5.6 reduce-precision_convert_fusion.3
  280.4 5.3 fusion.20
  292.8 5.6 reduce-precision_convert_fusion
  298.4 8.0 %copy.100 = bf16[2560,960]{1,0:T(8,128)(2,1)} copy(bf16[2560,960]{0,1:T(8,128)(2,1)} %reduce-precision_convert_fusion) | data formatting | bytes 9830400 | tf_op jit(solution)/shard_map/convert_element_type | solution.py:47
  316.7 7.3 %convolution_add_fusion = f32[768,960]{0,1:T(8,128)S(1)} fusion(f32[768,960]{0,1:T(8,128)} %fusion.20, bf16[768,2560]{1,0:T(8,128)(2,1)} %get-tuple-element.265, bf16[960,640]{1,0:T(8,128)(2,1)S(1)} %bitcast.179, bf16[960,640]{1,0:T(8,128)(2,1)} %bitcast.181, bf16[960,640]{1,0:T(8,128)(2,1)} %bitcast.183, bf16[960,640]{1,0:T(8,128)(2,1)S(1)} %bitcast.177), kind=kOutput, calls=%fused_computation.77 | convolution fusion | flops 3795271680 | bytes 14745600 | tf_op jit(solution)/shard_map/rb,ab->ra/dot_general | solution.py:264
  357.8 4.1 copy.104
  370.4 12.3 %shard_map.206 = (bf16[2,3,768,64]{3,2,1,0:T(8,128)(2,1)S(1)}, bf16[2,768,64]{2,1,0:T(8,128)(2,1)S(1)}, bf16[2,768,64]{2,1,0:T(8,128)(2,1)S(1)}) custom-call(bf16[5,3,768,64]{3,2,1,0:T(8,128)(2,1)S(1)} %maximum_bitcast_fusion.q_ref, bf16[5,768,64]{2,1,0:T(8,128)(2,1)S(1)} %copy-done.8, bf16[5,768,64]{2,1,0:T(8,128)(2,1)S(1)} %bitcast.124, ...), custom_call_target="tpu_custom_call" | custom-call | flops 9059696640 | bytes 16000000 | tf_op jit(solution)/shard_map/pallas_call | solution.py:379
  395.9 6.0 shard_map.207
  401.9 17.6 %collective-permute-done.33 = bf16[2,1,1,120,960]{4,3,2,1,0:T(8,128)(2,1)S(1)} collective-permute-done((bf16[2,1,1,120,960]{4,3,2,1,0:T(8,128)(2,1)S(1)}, bf16[2,1,1,120,960]{4,3,2,1,0:T(8,128)(2,1)S(1)}, u32[]{:S(2)}, u32[]{:S(2)}) %collective-permute-start.33) | collective-permute-done | bytes 460832 | tf_op jit(solution)/shard_map/ppermute | solution.py:29
  419.7 12.9 %collective-permute-done.32 = bf16[2,1,1,120,1280]{4,3,2,1,0:T(8,128)(2,1)S(1)} collective-permute-done((bf16[2,1,1,120,1280]{4,3,2,1,0:T(8,128)(2,1)S(1)}, bf16[2,1,1,120,1280]{4,3,2,1,0:T(8,128)(2,1)S(1)}, u32[]{:S(2)}, u32[]{:S(2)}) %collective-permute-start.32) | collective-permute-done | bytes 614432 | tf_op jit(solution)/shard_map/ppermute | solution.py:29
  432.9 11.1 %collective-permute-done.31 = bf16[2,1,1,120,1280]{4,3,2,1,0:T(8,128)(2,1)S(1)} collective-permute-done((bf16[2,1,1,120,1280]{4,3,2,1,0:T(8,128)(2,1)S(1)}, bf16[2,1,1,120,1280]{4,3,2,1,0:T(8,128)(2,1)S(1)}, u32[]{:S(2)}, u32[]{:S(2)}) %collective-permute-start.31) | collective-permute-done | bytes 614432 | tf_op jit(solution)/shard_map/ppermute | solution.py:29
  450.2 6.1 shard_map.208
  456.3 15.1 %collective-permute-done.37 = bf16[1,1,1,120,960]{4,3,2,1,0:T(8,128)(2,1)S(1)} collective-permute-done((bf16[1,1,1,120,960]{4,3,2,1,0:T(8,128)(2,1)S(1)}, bf16[1,1,1,120,960]{4,3,2,1,0:T(8,128)(2,1)S(1)}, u32[]{:S(2)}, u32[]{:S(2)}) %collective-permute-start.37) | collective-permute-done | bytes 230432 | tf_op jit(solution)/shard_map/ppermute | solution.py:29
  472.2 5.8 collective-permute-done.36
  478.8 4.4 collective-permute-done.35
  485.2 5.9 shard_map.209
  494.6 4.5 copy.109
  503.9 3.7 fusion.26
  507.6 5.0 fusion.12
  512.6 3.7 fusion.44
  525.3 3.7 fusion.46
  529.0 5.3 multiply_reduce_fusion.1
  534.6 8.5 %concatenate.183 = f32[2,2,2,120,1602]{4,3,2,1,0:T(8,128)} concatenate(f32[2,2,2,120,960]{4,3,2,1,0:T(8,128)} %fusion.44, f32[2,2,2,120,320]{4,3,2,1,0:T(8,128)} %fusion.45, f32[2,2,2,120,320]{4,3,2,1,0:T(8,128)} %fusion.46, f32[2,2,2,120,1]{4,3,2,1,0:T(8,128)S(1)} %concatenate.186, f32[2,2,2,120,1]{4,3,2,1,0:T(8,128)S(1)} %copy-done.71), dimensions={4} | concatenate | bytes 12303360 | tf_op jit(solution)/shard_map/concatenate | solution.py:585
  548.5 7.8 %multiply_convert_fusion.4 = bf16[768,960]{0,1:T(8,128)(2,1)} fusion(f32[768,960]{0,1:T(8,128)S(1)} %copy-done.36, bf16[768,2560]{1,0:T(8,128)(2,1)S(1)} %copy-done.114, bf16[2560,960]{1,0:T(8,128)(2,1)} %bitcast.156, f32[768]{0:T(1024)S(1)} %get-tuple-element.341), kind=kOutput, calls=%fused_computation.34 | convolution fusion | flops 3777085440 | bytes 13274112 | tf_op jit(solution)/shard_map/dot_general | solution.py:256
  566.7 11.8 %collective-permute-done.43 = bf16[2,1,1,120,1602]{4,3,2,1,0:T(8,128)(2,1)S(1)} collective-permute-done((bf16[2,1,1,120,1602]{4,3,2,1,0:T(8,128)(2,1)S(1)}, bf16[2,1,1,120,1602]{4,3,2,1,0:T(8,128)(2,1)S(1)}, u32[]{:S(2)}, u32[]{:S(2)}) %collective-permute-start.43) | collective-permute-done | bytes 768992 | tf_op jit(solution)/shard_map/ppermute | solution.py:29
  580.8 15.8 %collective-permute-done.44 = bf16[1,1,1,120,1602]{4,3,2,1,0:T(8,128)(2,1)S(1)} collective-permute-done((bf16[1,1,1,120,1602]{4,3,2,1,0:T(8,128)(2,1)S(1)}, bf16[1,1,1,120,1602]{4,3,2,1,0:T(8,128)(2,1)S(1)}, u32[]{:S(2)}, u32[]{:S(2)}) %collective-permute-start.44) | collective-permute-done | bytes 384512 | tf_op jit(solution)/shard_map/ppermute | solution.py:29
  597.4 10.3 %collective-permute-done.45 = bf16[120,1602]{1,0:T(8,128)(2,1)S(1)} collective-permute-done((bf16[120,1602]{1,0:T(8,128)(2,1)S(1)}, bf16[120,1602]{1,0:T(8,128)(2,1)S(1)}, u32[]{:S(2)}, u32[]{:S(2)}) %collective-permute-start.45) | collective-permute-done | bytes 384512 | tf_op jit(solution)/shard_map/ppermute | solution.py:29
  611.7 5.9 collective-permute-done.46
  (471 shorter events, 234.4 us)
Async XLA Ops:
  5.3 21.9 %collective-permute-start = (bf16[1,1,1,120,1602]{4,3,2,1,0:T(8,128)(2,1)S(1)}, bf16[1,1,1,120,1602]{4,3,2,1,0:T(8,128)(2,1)S(1)}, u32[]{:S(2)}, u32[]{:S(2)}) collective-permute-start(bf16[1,1,1,120,1602]{4,3,2,1,0:T(8,128)(2,1)S(1)} %bitcast.165), channel_id=1, source_target_pairs={{0,4},{1,5},{2,6},{3,7},{4,0},{5,1},{6,2},{7,3},{8,12},{9,13},{10,... | collective-permute-start | bytes 1153448 | tf_op jit(solution)/shard_map/ppermute | solution.py:29
  27.4 19.1 %collective-permute-start.1 = (bf16[2,1,1,120,1602]{4,3,2,1,0:T(8,128)(2,1)S(1)}, bf16[2,1,1,120,1602]{4,3,2,1,0:T(8,128)(2,1)S(1)}, u32[]{:S(2)}, u32[]{:S(2)}) collective-permute-start(bf16[2,1,1,120,1602]{4,3,2,1,0:T(8,128)(2,1)S(1)} %pad_maximum_fusion.19), channel_id=1, source_target_pairs={{0,2},{1,3},{2,0},{3,1},{4,6},{5,7},{6,4},{7,5},{8,10},{9,11},{10,... | collective-permute-start | bytes 2306888 | tf_op jit(solution)/shard_map/ppermute | solution.py:29
  63.5 35.5 %collective-permute-start.5 = (bf16[1,1,1,1,1,120,640]{6,5,4,3,2,1,0:T(8,128)(2,1)}, bf16[1,1,1,1,1,120,640]{6,5,4,3,2,1,0:T(8,128)(2,1)}, u32[]{:S(2)}, u32[]{:S(2)}) collective-permute-start(bf16[1,1,1,1,1,120,640]{6,5,4,3,2,1,0:T(8,128)(2,1)} %dynamic-slice_bitcast_fusion.1), channel_id=1, source_target_pairs={{0,4},{1,5},{2,6},{3,7},{4,0},{5,1},{6,2},{7,3},{8,12},{9,13},{10,... | collective-permute-start | bytes 460808 | tf_op jit(solution)/shard_map/ppermute | solution.py:29
  66.6 33.4 %collective-permute-start.4 = (bf16[1,1,1,1,1,120,640]{6,5,4,3,2,1,0:T(8,128)(2,1)}, bf16[1,1,1,1,1,120,640]{6,5,4,3,2,1,0:T(8,128)(2,1)}, u32[]{:S(2)}, u32[]{:S(2)}) collective-permute-start(bf16[1,1,1,1,1,120,640]{6,5,4,3,2,1,0:T(8,128)(2,1)} %dynamic-slice_bitcast_fusion.2), channel_id=1, source_target_pairs={{0,4},{1,5},{2,6},{3,7},{4,0},{5,1},{6,2},{7,3},{8,12},{9,13},{10,... | collective-permute-start | bytes 460808 | tf_op jit(solution)/shard_map/ppermute | solution.py:29
  68.2 32.9 %collective-permute-start.6 = (bf16[1,1,1,1,1,80,960]{6,5,4,3,2,1,0:T(8,128)(2,1)}, bf16[1,1,1,1,1,80,960]{6,5,4,3,2,1,0:T(8,128)(2,1)}, u32[]{:S(2)}, u32[]{:S(2)}) collective-permute-start(bf16[1,1,1,1,1,80,960]{6,5,4,3,2,1,0:T(8,128)(2,1)} %dynamic-slice_bitcast_fusion), channel_id=1, source_target_pairs={{0,4},{1,5},{2,6},{3,7},{4,0},{5,1},{6,2},{7,3},{8,12},{9,13},{10,... | collective-permute-start | bytes 460808 | tf_op jit(solution)/shard_map/ppermute | solution.py:29
  71.1 31.2 %collective-permute-start.3 = (bf16[1,1,1,120,960]{4,3,2,1,0:T(8,128)(2,1)S(1)}, bf16[1,1,1,120,960]{4,3,2,1,0:T(8,128)(2,1)}, u32[]{:S(2)}, u32[]{:S(2)}) collective-permute-start(bf16[1,1,1,120,960]{4,3,2,1,0:T(8,128)(2,1)S(1)} %bitcast.195), channel_id=1, source_target_pairs={{0,4},{1,5},{2,6},{3,7},{4,0},{5,1},{6,2},{7,3},{8,12},{9,13},{10,... | collective-permute-start | bytes 691208 | tf_op jit(solution)/shard_map/ppermute | solution.py:29
  103.5 10.3 %collective-permute-start.8 = (bf16[2,1,1,1,1,120,640]{6,5,4,3,2,1,0:T(8,128)(2,1)S(1)}, bf16[2,1,1,1,1,120,640]{6,5,4,3,2,1,0:T(8,128)(2,1)S(1)}, u32[]{:S(2)}, u32[]{:S(2)}) collective-permute-start(bf16[2,1,1,1,1,120,640]{6,5,4,3,2,1,0:T(8,128)(2,1)S(1)} %get-tuple-element.120), channel_id=1, source_target_pairs={{0,2},{1,3},{2,0},{3,1},{4,6},{5,7},{6,4},{7,5},{8,10},{9,11},{10,... | collective-permute-start | bytes 921608 | tf_op jit(solution)/shard_map/ppermute | solution.py:29
  105.8 14.5 %collective-permute-start.9 = (bf16[2,1,1,1,1,120,640]{6,5,4,3,2,1,0:T(8,128)(2,1)S(1)}, bf16[2,1,1,1,1,120,640]{6,5,4,3,2,1,0:T(8,128)(2,1)S(1)}, u32[]{:S(2)}, u32[]{:S(2)}) collective-permute-start(bf16[2,1,1,1,1,120,640]{6,5,4,3,2,1,0:T(8,128)(2,1)S(1)} %get-tuple-element.121), channel_id=1, source_target_pairs={{0,2},{1,3},{2,0},{3,1},{4,6},{5,7},{6,4},{7,5},{8,10},{9,11},{10,... | collective-permute-start | bytes 921608 | tf_op jit(solution)/shard_map/ppermute | solution.py:29
  106.2 16.0 %collective-permute-start.10 = (bf16[2,1,1,1,1,80,960]{6,5,4,3,2,1,0:T(8,128)(2,1)S(1)}, bf16[2,1,1,1,1,80,960]{6,5,4,3,2,1,0:T(8,128)(2,1)S(1)}, u32[]{:S(2)}, u32[]{:S(2)}) collective-permute-start(bf16[2,1,1,1,1,80,960]{6,5,4,3,2,1,0:T(8,128)(2,1)S(1)} %pad_maximum_fusion.26), channel_id=1, source_target_pairs={{0,16},{1,17},{2,18},{3,19},{4,20},{5,21},{6,22},{7,23},{8,24},{9,... | collective-permute-start | bytes 921608 | tf_op jit(solution)/shard_map/ppermute | solution.py:29
  107.7 21.8 %collective-permute-start.7 = (bf16[2,1,1,120,960]{4,3,2,1,0:T(8,128)(2,1)S(1)}, bf16[2,1,1,120,960]{4,3,2,1,0:T(8,128)(2,1)S(1)}, u32[]{:S(2)}, u32[]{:S(2)}) collective-permute-start(bf16[2,1,1,120,960]{4,3,2,1,0:T(8,128)(2,1)S(1)} %pad_maximum_fusion.23), channel_id=1, source_target_pairs={{0,2},{1,3},{2,0},{3,1},{4,6},{5,7},{6,4},{7,5},{8,10},{9,11},{10,... | collective-permute-start | bytes 1382408 | tf_op jit(solution)/shard_map/ppermute | solution.py:29
  130.6 15.6 %collective-permute-start.12 = (bf16[2,2,1,1,1,120,640]{6,5,4,3,2,1,0:T(8,128)(2,1)}, bf16[2,2,1,1,1,120,640]{6,5,4,3,2,1,0:T(8,128)(2,1)}, u32[]{:S(2)}, u32[]{:S(2)}) collective-permute-start(bf16[2,2,1,1,1,120,640]{6,5,4,3,2,1,0:T(8,128)(2,1)} %pad_maximum_fusion.21), channel_id=1, source_target_pairs={{0,16},{1,17},{2,18},{3,19},{4,20},{5,21},{6,22},{7,23},{8,24},{9,... | collective-permute-start | bytes 1843208 | tf_op jit(solution)/shard_map/ppermute | solution.py:29
  132.1 17.0 %collective-permute-start.13 = (bf16[2,2,1,1,1,120,640]{6,5,4,3,2,1,0:T(8,128)(2,1)}, bf16[2,2,1,1,1,120,640]{6,5,4,3,2,1,0:T(8,128)(2,1)S(1)}, u32[]{:S(2)}, u32[]{:S(2)}) collective-permute-start(bf16[2,2,1,1,1,120,640]{6,5,4,3,2,1,0:T(8,128)(2,1)} %pad_maximum_fusion.22), channel_id=1, source_target_pairs={{0,8},{1,9},{2,10},{3,11},{4,12},{5,13},{6,14},{7,15},{8,0},{9,1},... | collective-permute-start | bytes 1843208 | tf_op jit(solution)/shard_map/ppermute | solution.py:29
  133.6 27.0 %collective-permute-start.14 = (bf16[2,1,1,2,1,80,960]{6,5,4,3,2,1,0:T(8,128)(2,1)}, bf16[2,1,1,2,1,80,960]{6,5,4,3,2,1,0:T(8,128)(2,1)S(1)}, u32[]{:S(2)}, u32[]{:S(2)}) collective-permute-start(bf16[2,1,1,2,1,80,960]{6,5,4,3,2,1,0:T(8,128)(2,1)} %pad_maximum_fusion.20), channel_id=1, source_target_pairs={{0,8},{1,9},{2,10},{3,11},{4,12},{5,13},{6,14},{7,15},{8,0},{9,1},... | collective-permute-start | bytes 1843208 | tf_op jit(solution)/shard_map/ppermute | solution.py:29
  134.2 26.7 %collective-permute-start.11 = (bf16[2,2,1,120,960]{4,3,2,1,0:T(8,128)(2,1)}, bf16[2,2,1,120,960]{4,3,2,1,0:T(8,128)(2,1)S(1)}, u32[]{:S(2)}, u32[]{:S(2)}) collective-permute-start(bf16[2,2,1,120,960]{4,3,2,1,0:T(8,128)(2,1)} %pad_maximum_fusion.14), channel_id=1, source_target_pairs={{0,1},{1,0},{2,3},{3,2},{4,5},{5,4},{6,7},{7,6},{8,9},{9,8},{10,11... | collective-permute-start | bytes 2764808 | tf_op jit(solution)/shard_map/ppermute | solution.py:29
  162.5 26.5 %collective-permute-start.15 = (bf16[2,2,1,2,1,120,640]{6,5,4,3,2,1,0:T(8,128)(2,1)S(1)}, bf16[2,2,1,2,1,120,640]{6,5,4,3,2,1,0:T(8,128)(2,1)S(1)}, u32[]{:S(2)}, u32[]{:S(2)}) collective-permute-start(bf16[2,2,1,2,1,120,640]{6,5,4,3,2,1,0:T(8,128)(2,1)S(1)} %pad_maximum_fusion.12), channel_id=1, source_target_pairs={{0,8},{1,9},{2,10},{3,11},{4,12},{5,13},{6,14},{7,15},{8,0},{9,1},... | collective-permute-start | bytes 3686408 | tf_op jit(solution)/shard_map/ppermute | solution.py:29
  164.0 27.0 %collective-permute-start.16 = (bf16[2,2,1,1,2,120,640]{6,5,4,3,2,1,0:T(8,128)(2,1)S(1)}, bf16[2,2,1,1,2,120,640]{6,5,4,3,2,1,0:T(8,128)(2,1)S(1)}, u32[]{:S(2)}, u32[]{:S(2)}) collective-permute-start(bf16[2,2,1,1,2,120,640]{6,5,4,3,2,1,0:T(8,128)(2,1)S(1)} %pad_maximum_fusion.13), channel_id=1, source_target_pairs={{0,16},{1,17},{2,18},{3,19},{4,20},{5,21},{6,22},{7,23},{8,24},{9,... | collective-permute-start | bytes 3686408 | tf_op jit(solution)/shard_map/ppermute | solution.py:29
  164.5 28.5 %collective-permute-start.17 = (bf16[2,1,1,2,2,80,960]{6,5,4,3,2,1,0:T(8,128)(2,1)S(1)}, bf16[2,1,1,2,2,80,960]{6,5,4,3,2,1,0:T(8,128)(2,1)S(1)}, u32[]{:S(2)}, u32[]{:S(2)}) collective-permute-start(bf16[2,1,1,2,2,80,960]{6,5,4,3,2,1,0:T(8,128)(2,1)S(1)} %pad_maximum_fusion.11), channel_id=1, source_target_pairs={{0,2},{1,3},{2,0},{3,1},{4,6},{5,7},{6,4},{7,5},{8,10},{9,11},{10,... | collective-permute-start | bytes 3686408 | tf_op jit(solution)/shard_map/ppermute | solution.py:29
  194.9 32.8 %collective-permute-start.18 = (bf16[2,2,1,2,2,120,640]{6,5,4,3,2,1,0:T(8,128)(2,1)}, bf16[2,2,1,2,2,120,640]{6,5,4,3,2,1,0:T(8,128)(2,1)}, u32[]{:S(2)}, u32[]{:S(2)}) collective-permute-start(bf16[2,2,1,2,2,120,640]{6,5,4,3,2,1,0:T(8,128)(2,1)} %pad_maximum_fusion.7), channel_id=1, source_target_pairs={{0,1},{1,0},{2,3},{3,2},{4,5},{5,4},{6,7},{7,6},{8,9},{9,8},{10,11... | collective-permute-start | bytes 7372808 | tf_op jit(solution)/shard_map/ppermute | solution.py:29
  194.9 36.7 %collective-permute-start.19 = (bf16[2,2,1,2,2,120,640]{6,5,4,3,2,1,0:T(8,128)(2,1)}, bf16[2,2,1,2,2,120,640]{6,5,4,3,2,1,0:T(8,128)(2,1)}, u32[]{:S(2)}, u32[]{:S(2)}) collective-permute-start(bf16[2,2,1,2,2,120,640]{6,5,4,3,2,1,0:T(8,128)(2,1)} %pad_maximum_fusion.8), channel_id=1, source_target_pairs={{0,1},{1,0},{2,3},{3,2},{4,5},{5,4},{6,7},{7,6},{8,9},{9,8},{10,11... | collective-permute-start | bytes 7372808 | tf_op jit(solution)/shard_map/ppermute | solution.py:29
  221.4 16.5 %collective-permute-start.20 = (bf16[2,2,1,2,2,80,960]{6,5,4,3,2,1,0:T(8,128)(2,1)}, bf16[2,2,1,2,2,80,960]{6,5,4,3,2,1,0:T(8,128)(2,1)S(1)}, u32[]{:S(2)}, u32[]{:S(2)}) collective-permute-start(bf16[2,2,1,2,2,80,960]{6,5,4,3,2,1,0:T(8,128)(2,1)} %pad_maximum_fusion.6), channel_id=1, source_target_pairs={{0,1},{1,0},{2,3},{3,2},{4,5},{5,4},{6,7},{7,6},{8,9},{9,8},{10,11... | collective-permute-start | bytes 7372808 | tf_op jit(solution)/shard_map/ppermute | solution.py:29
  310.5 13.5 %collective-permute-start.24 = (bf16[2,2,1,120,1280]{4,3,2,1,0:T(8,128)(2,1)}, bf16[2,2,1,120,1280]{4,3,2,1,0:T(8,128)(2,1)}, u32[]{:S(2)}, u32[]{:S(2)}) collective-permute-start(bf16[2,2,1,120,1280]{4,3,2,1,0:T(8,128)(2,1)} %broadcast_select_fusion.16), channel_id=1, source_target_pairs={{0,1},{1,0},{2,3},{3,2},{4,5},{5,4},{6,7},{7,6},{8,9},{9,8},{10,11... | collective-permute-start | bytes 3686408 | tf_op jit(solution)/shard_map/ppermute | solution.py:29
  311.0 15.9 %collective-permute-start.25 = (bf16[2,2,1,120,1280]{4,3,2,1,0:T(8,128)(2,1)}, bf16[2,2,1,120,1280]{4,3,2,1,0:T(8,128)(2,1)}, u32[]{:S(2)}, u32[]{:S(2)}) collective-permute-start(bf16[2,2,1,120,1280]{4,3,2,1,0:T(8,128)(2,1)} %broadcast_select_fusion.15), channel_id=1, source_target_pairs={{0,1},{1,0},{2,3},{3,2},{4,5},{5,4},{6,7},{7,6},{8,9},{9,8},{10,11... | collective-permute-start | bytes 3686408 | tf_op jit(solution)/shard_map/ppermute | solution.py:29
  313.8 15.9 %collective-permute-start.22 = (bf16[2,2,1,120,1280]{4,3,2,1,0:T(8,128)(2,1)}, bf16[2,2,1,120,1280]{4,3,2,1,0:T(8,128)(2,1)}, u32[]{:S(2)}, u32[]{:S(2)}) collective-permute-start(bf16[2,2,1,120,1280]{4,3,2,1,0:T(8,128)(2,1)} %broadcast_select_fusion.18), channel_id=1, source_target_pairs={{0,1},{1,0},{2,3},{3,2},{4,5},{5,4},{6,7},{7,6},{8,9},{9,8},{10,11... | collective-permute-start | bytes 3686408 | tf_op jit(solution)/shard_map/ppermute | solution.py:29
  314.3 18.2 %collective-permute-start.23 = (bf16[2,2,1,120,1280]{4,3,2,1,0:T(8,128)(2,1)}, bf16[2,2,1,120,1280]{4,3,2,1,0:T(8,128)(2,1)S(1)}, u32[]{:S(2)}, u32[]{:S(2)}) collective-permute-start(bf16[2,2,1,120,1280]{4,3,2,1,0:T(8,128)(2,1)} %broadcast_select_fusion.17), channel_id=1, source_target_pairs={{0,1},{1,0},{2,3},{3,2},{4,5},{5,4},{6,7},{7,6},{8,9},{9,8},{10,11... | collective-permute-start | bytes 3686408 | tf_op jit(solution)/shard_map/ppermute | solution.py:29
  315.4 18.6 %collective-permute-start.21 = (bf16[2,2,1,320,960]{4,3,2,1,0:T(8,128)(2,1)S(1)}, bf16[2,2,1,320,960]{4,3,2,1,0:T(8,128)(2,1)S(1)}, u32[]{:S(2)}, u32[]{:S(2)}) collective-permute-start(bf16[2,2,1,320,960]{4,3,2,1,0:T(8,128)(2,1)S(1)} %broadcast_select_fusion), channel_id=1, source_target_pairs={{0,1},{1,0},{2,3},{3,2},{4,5},{5,4},{6,7},{7,6},{8,9},{9,8},{10,11... | collective-permute-start | bytes 7372808 | tf_op jit(solution)/shard_map/ppermute | solution.py:29
  350.0 32.8 %collective-permute-start.29 = (bf16[2,2,1,120,960]{4,3,2,1,0:T(8,128)(2,1)}, bf16[2,2,1,120,960]{4,3,2,1,0:T(8,128)(2,1)}, u32[]{:S(2)}, u32[]{:S(2)}) collective-permute-start(bf16[2,2,1,120,960]{4,3,2,1,0:T(8,128)(2,1)} %broadcast_select_fusion.23), channel_id=1, source_target_pairs={{0,1},{1,0},{2,3},{3,2},{4,5},{5,4},{6,7},{7,6},{8,9},{9,8},{10,11... | collective-permute-start | bytes 2764808 | tf_op jit(solution)/shard_map/ppermute | solution.py:29
  351.6 33.3 %collective-permute-start.28 = (bf16[2,2,1,120,1280]{4,3,2,1,0:T(8,128)(2,1)}, bf16[2,2,1,120,1280]{4,3,2,1,0:T(8,128)(2,1)}, u32[]{:S(2)}, u32[]{:S(2)}) collective-permute-start(bf16[2,2,1,120,1280]{4,3,2,1,0:T(8,128)(2,1)} %broadcast_select_fusion.13), channel_id=1, source_target_pairs={{0,8},{1,9},{2,10},{3,11},{4,12},{5,13},{6,14},{7,15},{8,0},{9,1},... | collective-permute-start | bytes 3686408 | tf_op jit(solution)/shard_map/ppermute | solution.py:29
  354.3 32.6 %collective-permute-start.27 = (bf16[2,2,1,120,1280]{4,3,2,1,0:T(8,128)(2,1)}, bf16[2,2,1,120,1280]{4,3,2,1,0:T(8,128)(2,1)}, u32[]{:S(2)}, u32[]{:S(2)}) collective-permute-start(bf16[2,2,1,120,1280]{4,3,2,1,0:T(8,128)(2,1)} %broadcast_select_fusion.14), channel_id=1, source_target_pairs={{0,16},{1,17},{2,18},{3,19},{4,20},{5,21},{6,22},{7,23},{8,24},{9,... | collective-permute-start | bytes 3686408 | tf_op jit(solution)/shard_map/ppermute | solution.py:29
  356.0 32.8 %collective-permute-start.26 = (bf16[2,1,1,320,960]{4,3,2,1,0:T(8,128)(2,1)}, bf16[2,1,1,320,960]{4,3,2,1,0:T(8,128)(2,1)}, u32[]{:S(2)}, u32[]{:S(2)}) collective-permute-start(bf16[2,1,1,320,960]{4,3,2,1,0:T(8,128)(2,1)} %broadcast_select_fusion.10), channel_id=1, source_target_pairs={{0,2},{1,3},{2,0},{3,1},{4,6},{5,7},{6,4},{7,5},{8,10},{9,11},{10,... | collective-permute-start | bytes 3686408 | tf_op jit(solution)/shard_map/ppermute | solution.py:29
  391.2 28.3 %collective-permute-start.33 = (bf16[2,1,1,120,960]{4,3,2,1,0:T(8,128)(2,1)S(1)}, bf16[2,1,1,120,960]{4,3,2,1,0:T(8,128)(2,1)S(1)}, u32[]{:S(2)}, u32[]{:S(2)}) collective-permute-start(bf16[2,1,1,120,960]{4,3,2,1,0:T(8,128)(2,1)S(1)} %broadcast_select_fusion.38), channel_id=1, source_target_pairs={{0,2},{1,3},{2,0},{3,1},{4,6},{5,7},{6,4},{7,5},{8,10},{9,11},{10,... | collective-permute-start | bytes 1382408 | tf_op jit(solution)/shard_map/ppermute | solution.py:29
  391.7 41.0 %collective-permute-start.32 = (bf16[2,1,1,120,1280]{4,3,2,1,0:T(8,128)(2,1)S(1)}, bf16[2,1,1,120,1280]{4,3,2,1,0:T(8,128)(2,1)S(1)}, u32[]{:S(2)}, u32[]{:S(2)}) collective-permute-start(bf16[2,1,1,120,1280]{4,3,2,1,0:T(8,128)(2,1)S(1)} %broadcast_select_fusion.32), channel_id=1, source_target_pairs={{0,2},{1,3},{2,0},{3,1},{4,6},{5,7},{6,4},{7,5},{8,10},{9,11},{10,... | collective-permute-start | bytes 1843208 | tf_op jit(solution)/shard_map/ppermute | solution.py:29
  393.5 50.5 %collective-permute-start.31 = (bf16[2,1,1,120,1280]{4,3,2,1,0:T(8,128)(2,1)S(1)}, bf16[2,1,1,120,1280]{4,3,2,1,0:T(8,128)(2,1)S(1)}, u32[]{:S(2)}, u32[]{:S(2)}) collective-permute-start(bf16[2,1,1,120,1280]{4,3,2,1,0:T(8,128)(2,1)S(1)} %broadcast_select_fusion.33), channel_id=1, source_target_pairs={{0,2},{1,3},{2,0},{3,1},{4,6},{5,7},{6,4},{7,5},{8,10},{9,11},{10,... | collective-permute-start | bytes 1843208 | tf_op jit(solution)/shard_map/ppermute | solution.py:29
  393.9 50.3 %collective-permute-start.30 = (bf16[1,1,1,320,960]{4,3,2,1,0:T(8,128)(2,1)S(1)}, bf16[1,1,1,320,960]{4,3,2,1,0:T(8,128)(2,1)S(1)}, u32[]{:S(2)}, u32[]{:S(2)}) collective-permute-start(bf16[1,1,1,320,960]{4,3,2,1,0:T(8,128)(2,1)S(1)} %broadcast_select_fusion.29), channel_id=1, source_target_pairs={{0,4},{1,5},{2,6},{3,7},{4,0},{5,1},{6,2},{7,3},{8,12},{9,13},{10,... | collective-permute-start | bytes 1843208 | tf_op jit(solution)/shard_map/ppermute | solution.py:29
  444.6 26.8 %collective-permute-start.37 = (bf16[1,1,1,120,960]{4,3,2,1,0:T(8,128)(2,1)S(1)}, bf16[1,1,1,120,960]{4,3,2,1,0:T(8,128)(2,1)S(1)}, u32[]{:S(2)}, u32[]{:S(2)}) collective-permute-start(bf16[1,1,1,120,960]{4,3,2,1,0:T(8,128)(2,1)S(1)} %broadcast_select_fusion.56), channel_id=1, source_target_pairs={{0,4},{1,5},{2,6},{3,7},{4,0},{5,1},{6,2},{7,3},{8,12},{9,13},{10,... | collective-permute-start | bytes 691208 | tf_op jit(solution)/shard_map/ppermute | solution.py:29
  445.7 32.3 %collective-permute-start.36 = (bf16[1,1,1,120,1280]{4,3,2,1,0:T(8,128)(2,1)S(1)}, bf16[1,1,1,120,1280]{4,3,2,1,0:T(8,128)(2,1)S(1)}, u32[]{:S(2)}, u32[]{:S(2)}) collective-permute-start(bf16[1,1,1,120,1280]{4,3,2,1,0:T(8,128)(2,1)S(1)} %broadcast_select_fusion.50), channel_id=1, source_target_pairs={{0,4},{1,5},{2,6},{3,7},{4,0},{5,1},{6,2},{7,3},{8,12},{9,13},{10,... | collective-permute-start | bytes 921608 | tf_op jit(solution)/shard_map/ppermute | solution.py:29
  447.7 35.5 %collective-permute-start.35 = (bf16[1,1,1,120,1280]{4,3,2,1,0:T(8,128)(2,1)S(1)}, bf16[1,1,1,120,1280]{4,3,2,1,0:T(8,128)(2,1)S(1)}, u32[]{:S(2)}, u32[]{:S(2)}) collective-permute-start(bf16[1,1,1,120,1280]{4,3,2,1,0:T(8,128)(2,1)S(1)} %broadcast_select_fusion.51), channel_id=1, source_target_pairs={{0,4},{1,5},{2,6},{3,7},{4,0},{5,1},{6,2},{7,3},{8,12},{9,13},{10,... | collective-permute-start | bytes 921608 | tf_op jit(solution)/shard_map/ppermute | solution.py:29
  448.7 35.4 %collective-permute-start.34 = (bf16[320,960]{1,0:T(8,128)(2,1)S(1)}, bf16[320,960]{1,0:T(8,128)(2,1)S(1)}, u32[]{:S(2)}, u32[]{:S(2)}) collective-permute-start(bf16[320,960]{1,0:T(8,128)(2,1)S(1)} %bitcast.158), channel_id=1, source_target_pairs={{0,16},{1,17},{2,18},{3,19},{4,20},{5,21},{6,22},{7,23},{8,24},{9,... | collective-permute-start | bytes 1843208 | tf_op jit(solution)/shard_map/ppermute | solution.py:29
  499.8 18.5 %collective-permute-start.41 = (bf16[120,960]{1,0:T(8,128)(2,1)}, bf16[120,960]{1,0:T(8,128)(2,1)S(1)}, u32[]{:S(2)}, u32[]{:S(2)}) collective-permute-start(bf16[120,960]{1,0:T(8,128)(2,1)} %bitcast.193), channel_id=1, source_target_pairs={{0,16},{1,17},{2,18},{3,19},{4,20},{5,21},{6,22},{7,23},{8,24},{9,... | collective-permute-start | bytes 691208 | tf_op jit(solution)/shard_map/ppermute | solution.py:29
  501.3 17.8 %collective-permute-start.40 = (bf16[120,1280]{1,0:T(8,128)(2,1)}, bf16[120,1280]{1,0:T(8,128)(2,1)S(1)}, u32[]{:S(2)}, u32[]{:S(2)}) collective-permute-start(bf16[120,1280]{1,0:T(8,128)(2,1)} %bitcast.174), channel_id=1, source_target_pairs={{0,16},{1,17},{2,18},{3,19},{4,20},{5,21},{6,22},{7,23},{8,24},{9,... | collective-permute-start | bytes 921608 | tf_op jit(solution)/shard_map/ppermute | solution.py:29
  501.9 18.0 %collective-permute-start.39 = (bf16[120,1280]{1,0:T(8,128)(2,1)}, bf16[120,1280]{1,0:T(8,128)(2,1)S(1)}, u32[]{:S(2)}, u32[]{:S(2)}) collective-permute-start(bf16[120,1280]{1,0:T(8,128)(2,1)} %bitcast.175), channel_id=1, source_target_pairs={{0,8},{1,9},{2,10},{3,11},{4,12},{5,13},{6,14},{7,15},{8,0},{9,1},... | collective-permute-start | bytes 921608 | tf_op jit(solution)/shard_map/ppermute | solution.py:29
  503.6 20.0 %collective-permute-start.38 = (bf16[320,960]{1,0:T(8,128)(2,1)S(1)}, bf16[320,960]{1,0:T(8,128)(2,1)S(1)}, u32[]{:S(2)}, u32[]{:S(2)}) collective-permute-start(bf16[320,960]{1,0:T(8,128)(2,1)S(1)} %copy-done.69), channel_id=1, source_target_pairs={{0,8},{1,9},{2,10},{3,11},{4,12},{5,13},{6,14},{7,15},{8,0},{9,1},... | collective-permute-start | bytes 1843208 | tf_op jit(solution)/shard_map/ppermute | solution.py:29
  546.7 13.2 %collective-permute-start.42 = (bf16[2,2,1,120,1602]{4,3,2,1,0:T(8,128)(2,1)S(1)}, bf16[2,2,1,120,1602]{4,3,2,1,0:T(8,128)(2,1)S(1)}, u32[]{:S(2)}, u32[]{:S(2)}) collective-permute-start(bf16[2,2,1,120,1602]{4,3,2,1,0:T(8,128)(2,1)S(1)} %broadcast_select_fusion.7), channel_id=1, source_target_pairs={{0,1},{1,0},{2,3},{3,2},{4,5},{5,4},{6,7},{7,6},{8,9},{9,8},{10,11... | collective-permute-start | bytes 4613768 | tf_op jit(solution)/shard_map/ppermute | solution.py:29
  558.0 22.8 %collective-permute-start.48 = (bf16[120,1280]{1,0:T(8,128)(2,1)S(1)}, bf16[120,1280]{1,0:T(8,128)(2,1)S(1)}, u32[]{:S(2)}, u32[]{:S(2)}) collective-permute-start(bf16[120,1280]{1,0:T(8,128)(2,1)S(1)} %copy-done.84), channel_id=1, source_target_pairs={{0,16},{1,17},{2,18},{3,19},{4,20},{5,21},{6,22},{7,23},{8,24},{9,... | collective-permute-start | bytes 921608 | tf_op jit(solution)/shard_map/ppermute | solution.py:29
  559.6 37.7 %collective-permute-start.49 = (bf16[120,1280]{1,0:T(8,128)(2,1)S(1)}, bf16[120,1280]{1,0:T(8,128)(2,1)S(1)}, u32[]{:S(2)}, u32[]{:S(2)}) collective-permute-start(bf16[120,1280]{1,0:T(8,128)(2,1)S(1)} %copy-done.83), channel_id=1, source_target_pairs={{0,8},{1,9},{2,10},{3,11},{4,12},{5,13},{6,14},{7,15},{8,0},{9,1},... | collective-permute-start | bytes 921608 | tf_op jit(solution)/shard_map/ppermute | solution.py:29
  560.7 17.8 %collective-permute-start.43 = (bf16[2,1,1,120,1602]{4,3,2,1,0:T(8,128)(2,1)S(1)}, bf16[2,1,1,120,1602]{4,3,2,1,0:T(8,128)(2,1)S(1)}, u32[]{:S(2)}, u32[]{:S(2)}) collective-permute-start(bf16[2,1,1,120,1602]{4,3,2,1,0:T(8,128)(2,1)S(1)} %broadcast_select_fusion.26), channel_id=1, source_target_pairs={{0,2},{1,3},{2,0},{3,1},{4,6},{5,7},{6,4},{7,5},{8,10},{9,11},{10,... | collective-permute-start | bytes 2306888 | tf_op jit(solution)/shard_map/ppermute | solution.py:29
  578.9 17.8 %collective-permute-start.44 = (bf16[1,1,1,120,1602]{4,3,2,1,0:T(8,128)(2,1)S(1)}, bf16[1,1,1,120,1602]{4,3,2,1,0:T(8,128)(2,1)S(1)}, u32[]{:S(2)}, u32[]{:S(2)}) collective-permute-start(bf16[1,1,1,120,1602]{4,3,2,1,0:T(8,128)(2,1)S(1)} %broadcast_select_fusion.41), channel_id=1, source_target_pairs={{0,4},{1,5},{2,6},{3,7},{4,0},{5,1},{6,2},{7,3},{8,12},{9,13},{10,... | collective-permute-start | bytes 1153448 | tf_op jit(solution)/shard_map/ppermute | solution.py:29
  596.8 10.8 %collective-permute-start.45 = (bf16[120,1602]{1,0:T(8,128)(2,1)S(1)}, bf16[120,1602]{1,0:T(8,128)(2,1)S(1)}, u32[]{:S(2)}, u32[]{:S(2)}) collective-permute-start(bf16[120,1602]{1,0:T(8,128)(2,1)S(1)} %fusion.30), channel_id=1, source_target_pairs={{0,16},{1,17},{2,18},{3,19},{4,20},{5,21},{6,22},{7,23},{8,24},{9,... | collective-permute-start | bytes 1153448 | tf_op jit(solution)/shard_map/ppermute | solution.py:29
  607.8 9.9 %collective-permute-start.46 = (bf16[120,1602]{1,0:T(8,128)(2,1)S(1)}, bf16[120,1602]{1,0:T(8,128)(2,1)S(1)}, u32[]{:S(2)}, u32[]{:S(2)}) collective-permute-start(bf16[120,1602]{1,0:T(8,128)(2,1)S(1)} %reduce-precision_convert_fusion.25), channel_id=1, source_target_pairs={{0,8},{1,9},{2,10},{3,11},{4,12},{5,13},{6,14},{7,15},{8,0},{9,1},... | collective-permute-start | bytes 1153448 | tf_op jit(solution)/shard_map/ppermute | solution.py:29
  (117 other events, 765.2 us)
